TPU v7x, 128 devices: a whole 4x4x4 slice. The times are simulated.
128 devices in a mesh: seq: 8 (over z, y_hi), batch: 16 (over y_lo, x, core).
Axes of the slice: x: 4, y: 4 (y_hi: 2, y_lo: 2; y = y_hi * 2 + y_lo), z: 4, core: 2. Of those that a mesh axis runs over, the one named last changes fastest.
Arguments:
- queries: bfloat16 [16, 1536, 2048], P('batch', 'seq'), may hold values from -16 to 16
- key_vectors: bfloat16 [16, 1536, 2048], P('batch', 'seq'), may hold values from -16 to 16
- value_vectors: bfloat16 [16, 1536, 2048], P('batch', 'seq'), may hold values from -6 to 6
- cotangent: bfloat16 [16, 1536, 2048], P('batch', 'seq'), may hold values from -6 to 6
- clip_raw: bfloat16 [2048, 768], P(('seq', 'batch')), may hold values from -0.3984375 to 0.3984375
- text_raw: bfloat16 [2048, 768], P(('seq', 'batch')), may hold values from -0.3984375 to 0.3984375
- clip_video: int32 [2048], P(('seq', 'batch')), may hold values from 0 to 511
- text_video: int32 [2048], P(('seq', 'batch')), may hold values from 0 to 511
- logit_scale: float32 [1], replicated, may hold values from 5 to 15
- logit_bias: float32 [1], replicated, may hold values from -8 to -4
Outputs:
- attended: bfloat16 [16, 1536, 2048], P('batch', 'seq')
- grad_queries: bfloat16 [16, 1536, 2048], P('batch', 'seq')
- grad_keys: bfloat16 [16, 1536, 2048], P('batch', 'seq')
- grad_values: bfloat16 [16, 1536, 2048], P('batch', 'seq')
- grad_clip: float32 [2048, 768], P(('seq', 'batch'))
- grad_text: float32 [2048, 768], P(('seq', 'batch'))
- loss_mean: float32 [1], replicated
All inputs are finite; a program needn't handle non-finite values.
Results may differ from a plain program's by a relative error of at most 0.0098.
The roundings to bfloat16 on the way count: a program that leaves them out, or rounds other values in their place, can miss the bound.
Values may be sent and summed in bfloat16 or wider, within the bound.
A program may use at most 64 MiB of HBM per device.

v0:
```python
import math

import jax
import jax.numpy as jnp
from jax import lax
from jax.sharding import PartitionSpec as P

HD = 128


def unit_rows(raw):
    rawf = raw.astype(jnp.float32)
    norm = jnp.sqrt(jnp.sum(rawf * rawf, axis=1, keepdims=True) + 1e-06)
    return (rawf / norm, norm)


def raw_grad(unit, norm, direction):
    return (direction - unit * jnp.sum(unit * direction, axis=1, keepdims=True)) / norm


def body(
    queries,
    key_vectors,
    value_vectors,
    cotangent,
    clip_raw,
    text_raw,
    clip_video,
    text_video,
    logit_scale,
    logit_bias,
):
    tokens_here = queries.shape[1]
    width = queries.shape[2]
    head_dim = HD
    heads = width // head_dim
    inv_root = 1.0 / math.sqrt(head_dim)

    def split_heads(array):
        return array.reshape(tokens_here, heads, head_dim)

    q_heads, k_heads, v_heads = (
        lax.all_to_all(split_heads(queries), "seq", split_axis=1, concat_axis=0, tiled=True),
        lax.all_to_all(split_heads(key_vectors), "seq", split_axis=1, concat_axis=0, tiled=True),
        lax.all_to_all(split_heads(value_vectors), "seq", split_axis=1, concat_axis=0, tiled=True),
    )
    full = q_heads.shape[0]
    local_heads = q_heads.shape[1]
    block = math.gcd(512, full)
    blocks = full // block

    def in_blocks(array):
        return array.reshape(blocks, block, local_heads, head_dim)

    def block_scores(q_block):
        return (
            jnp.einsum("qhd,khd->hqk", q_block, k_heads, preferred_element_type=jnp.float32)
            * inv_root
        )

    def forward_block(q_block):
        scores = block_scores(q_block)
        top = jnp.max(scores, axis=2, keepdims=True)
        expo = jnp.exp(scores - top)
        total = jnp.sum(expo, axis=2, keepdims=True)
        probs_b = (expo / total).astype(jnp.bfloat16)
        out_block = jnp.einsum(
            "hqk,khd->qhd", probs_b, v_heads, preferred_element_type=jnp.float32
        ).astype(jnp.bfloat16)
        return (out_block, top, total)

    q_blocks = in_blocks(q_heads)
    out_blocks, tops, totals = lax.map(forward_block, q_blocks)
    out_heads = out_blocks.reshape(full, local_heads, head_dim)
    attended_rows = lax.all_to_all(out_heads, "seq", split_axis=0, concat_axis=1, tiled=True)
    d_heads = lax.all_to_all(split_heads(cotangent), "seq", split_axis=1, concat_axis=0, tiled=True)

    def backward_block(carry, items):
        key_sum, value_sum = carry
        q_block, d_block, o_block, top, total = items
        probs = jnp.exp(block_scores(q_block) - top) / total
        probs_b = probs.astype(jnp.bfloat16)
        value_part = jnp.einsum(
            "hqk,qhd->khd", probs_b, d_block, preferred_element_type=jnp.float32
        )
        dprobs = jnp.einsum("qhd,khd->hqk", d_block, v_heads, preferred_element_type=jnp.float32)
        delta = jnp.sum(d_block.astype(jnp.float32) * o_block.astype(jnp.float32), axis=2)
        dscores = (probs * (dprobs - jnp.transpose(delta)[:, :, None])).astype(jnp.bfloat16)
        q_grad = (
            jnp.einsum("hqk,khd->qhd", dscores, k_heads, preferred_element_type=jnp.float32)
            * inv_root
        ).astype(jnp.bfloat16)
        key_part = jnp.einsum("hqk,qhd->khd", dscores, q_block, preferred_element_type=jnp.float32)
        return ((key_sum + key_part, value_sum + value_part), q_grad)

    zeros_heads = jnp.zeros((full, local_heads, head_dim), jnp.float32)
    (key_sum, value_sum), q_grads = lax.scan(
        backward_block,
        (zeros_heads, zeros_heads),
        (q_blocks, in_blocks(d_heads), out_blocks, tops, totals),
    )
    dq_heads = q_grads.reshape(full, local_heads, head_dim)
    dk_heads = (key_sum * inv_root).astype(jnp.bfloat16)
    dv_heads = value_sum.astype(jnp.bfloat16)
    dq_rows, dk_rows, dv_rows = (
        lax.all_to_all(dq_heads, "seq", split_axis=0, concat_axis=1, tiled=True),
        lax.all_to_all(dk_heads, "seq", split_axis=0, concat_axis=1, tiled=True),
        lax.all_to_all(dv_heads, "seq", split_axis=0, concat_axis=1, tiled=True),
    )

    def merge_heads(array):
        return array.reshape(1, tokens_here, width)

    clip_unit, clip_norm = unit_rows(clip_raw)
    text_unit, text_norm = unit_rows(text_raw)
    clip_b = clip_unit.astype(jnp.bfloat16)
    text_b = text_unit.astype(jnp.bfloat16)
    scale = logit_scale[0]
    offset = logit_bias[0]
    texts_here = text_raw.shape[0]
    rows_all = texts_here * lax.axis_size(("seq", "batch"))
    empty_total = jnp.zeros((), jnp.float32)
    piece = (
        lax.all_gather(text_b, ("seq", "batch"), axis=0, tiled=True),
        lax.all_gather(text_video, ("seq", "batch"), axis=0, tiled=True),
    )
    total = empty_total
    logits = (
        scale
        * lax.dot_general(
            clip_b, piece[0], (((1,), (1,)), ((), ())), preferred_element_type=jnp.float32
        )
        + offset
    )
    sign = jnp.where(clip_video[:, None] == piece[1][None, :], jnp.float32(1.0), jnp.float32(-1.0))
    pair_grad = (scale * -sign * jax.nn.sigmoid(-sign * logits)).astype(jnp.bfloat16)
    pair_grad, part = (pair_grad, jnp.sum(jax.nn.softplus(-sign * logits)))
    clip_acc = jnp.dot(pair_grad, piece[0], preferred_element_type=jnp.float32)
    total = part
    text_dir = lax.psum_scatter(
        lax.dot_general(
            pair_grad, clip_b, (((0,), (0,)), ((), ())), preferred_element_type=jnp.float32
        ),
        ("seq", "batch"),
        scatter_dimension=0,
        tiled=True,
    )
    loss_sum = lax.psum(total, ("seq", "batch"))
    loss_mean = jnp.reshape(loss_sum / rows_all, (1,))
    grad_clip = raw_grad(clip_unit, clip_norm, clip_acc)
    grad_text = raw_grad(text_unit, text_norm, text_dir)
    return (
        merge_heads(attended_rows),
        merge_heads(dq_rows),
        merge_heads(dk_rows),
        merge_heads(dv_rows),
        grad_clip,
        grad_text,
        loss_mean,
    )


def solution(mesh):
    in_specs = (
        P("batch", "seq", None),
        P("batch", "seq", None),
        P("batch", "seq", None),
        P("batch", "seq", None),
        P(("seq", "batch"), None),
        P(("seq", "batch"), None),
        P(("seq", "batch")),
        P(("seq", "batch")),
        P(),
        P(),
    )
    out_specs = (
        P("batch", "seq", None),
        P("batch", "seq", None),
        P("batch", "seq", None),
        P("batch", "seq", None),
        P(("seq", "batch"), None),
        P(("seq", "batch"), None),
        P(),
    )
    return jax.shard_map(body, mesh=mesh, in_specs=in_specs, out_specs=out_specs, check_vma=False)
```

profile of v0, /device:TPU:0, one launch (start us, length us, event | category | flops | bytes accessed | tf_op | source)
XLA Modules:
  0.0 406.5 jit_solution(7996264941817297749)
XLA Ops:
  7.2 1.4 copy.130
  8.5 1.1 copy.99
  9.6 8.2 %all-to-all-start = ((bf16[192,16,128]{2,0,1:T(8,128)(2,1)}), bf16[192,16,128]{2,0,1:T(8,128)(2,1)S(1)}, u32[]{:S(2)}, u32[]{:S(2)}) async-start(bf16[192,16,128]{2,0,1:T(8,128)(2,1)} %copy.99), calls=%async_computation | async-start | bytes 1572864 | tf_op jit(solution)/shard_map/all_to_all | solution.py:43
  18.0 1.1 copy.101
  19.1 13.1 %all-to-all-done = bf16[192,16,128]{2,0,1:T(8,128)(2,1)S(1)} async-done(((bf16[192,16,128]{2,0,1:T(8,128)(2,1)}), bf16[192,16,128]{2,0,1:T(8,128)(2,1)S(1)}, u32[]{:S(2)}, u32[]{:S(2)}) %all-to-all-start) | async-done | bytes 786464 | tf_op jit(solution)/shard_map/all_to_all | solution.py:43
  32.2 3.5 all-to-all-start.1
  35.9 1.1 copy.103
  37.0 12.2 %all-to-all-done.1 = bf16[192,16,128]{2,0,1:T(8,128)(2,1)S(1)} async-done(((bf16[192,16,128]{2,0,1:T(8,128)(2,1)}), bf16[192,16,128]{2,0,1:T(8,128)(2,1)S(1)}, u32[]{:S(2)}, u32[]{:S(2)}) %all-to-all-start.1) | async-done | bytes 786464 | tf_op jit(solution)/shard_map/all_to_all | solution.py:44
  49.2 3.5 all-to-all-start.2
  52.9 1.1 copy.110
  54.1 11.1 %all-to-all-done.2 = bf16[192,16,128]{2,0,1:T(8,128)(2,1)S(1)} async-done(((bf16[192,16,128]{2,0,1:T(8,128)(2,1)}), bf16[192,16,128]{2,0,1:T(8,128)(2,1)S(1)}, u32[]{:S(2)}, u32[]{:S(2)}) %all-to-all-start.2) | async-done | bytes 786464 | tf_op jit(solution)/shard_map/all_to_all | solution.py:45
  65.3 4.2 %all-to-all-start.4 = ((bf16[192,16,128]{2,0,1:T(8,128)(2,1)}), bf16[192,16,128]{2,0,1:T(8,128)(2,1)}, u32[]{:S(2)}, u32[]{:S(2)}) async-start(bf16[192,16,128]{2,0,1:T(8,128)(2,1)} %copy.110), calls=%async_computation.4 | async-start | bytes 1572864 | tf_op jit(solution)/shard_map/all_to_all | solution.py:76
  72.1 66.0 %all-reduce = s32[2048]{0:T(1024)S(1)} all-reduce(s32[2048]{0:T(1024)S(1)} %dynamic-update-slice), channel_id=1, replica_groups=mesh['seq'=8,'batch'=16] {'seq','batch'}, use_global_device_ids=true, to_apply=%add | all-reduce | flops 2048 | bytes 16384
  138.1 1.3 copy.100
  142.2 2.1 copy.111
  144.3 17.4 %while.29 = (s32[]{:T(128)}, bf16[3,512,2,128]{3,1,2,0:T(8,128)(2,1)}, f32[3,2,512,1]{2,1,3,0:T(2,128)S(1)}, f32[3,2,512,1]{2,1,3,0:T(2,128)S(1)}, bf16[3,512,2,...) while((s32[]{:T(128)}, ...), condition=%wide.region_3.4_spmd, body=%wide.region_0.3_spmd.sunk | while | flops 819591168 | bytes 24154244 | solution.py:73
  144.3 2.3 multiply_reduce_fusion.4
  146.6 1.2 fusion.74
  147.8 2.3 fusion.75
  150.1 2.3 multiply_reduce_fusion.4
  152.4 1.2 fusion.74
  153.6 2.3 fusion.75
  155.9 2.3 multiply_reduce_fusion.4
  158.2 1.2 fusion.74
  159.3 2.3 fusion.75
  161.7 1.2 copy.106
  162.9 7.3 %copy.107 = bf16[1536,2,128]{2,1,0:T(2,128)(2,1)} copy(bf16[1536,2,128]{2,0,1:T(8,128)(2,1)S(1)} %bitcast.167) | data formatting | bytes 1572864 | tf_op jit(solution)/shard_map/reshape | solution.py:74
  170.1 4.5 %all-to-all-start.3 = ((bf16[1536,2,128]{2,1,0:T(2,128)(2,1)}), bf16[1536,2,128]{2,1,0:T(2,128)(2,1)}, u32[]{:S(2)}, u32[]{:S(2)}) async-start(bf16[1536,2,128]{2,1,0:T(2,128)(2,1)} %copy.107), calls=%async_computation.3 | async-start | bytes 1572864 | tf_op jit(solution)/shard_map/all_to_all | solution.py:75
  174.9 3.5 fusion.37
  178.4 3.8 fusion.40
  182.1 29.6 %while.30 = (s32[]{:T(128)}, f32[1536,2,128]{0,2,1:T(8,128)S(1)}, f32[1536,2,128]{0,2,1:T(8,128)S(1)}, bf16[3,512,2,128]{3,1,0,2:T(8,128)(2,1)}, bf16[3,512,2,12...) while((s32[]{:T(128)}, f32[1536,2,128]{0,2,1:T(8,128)S(1)}, ...), condition=%wide.region_6.7_spmd.clone, body=%wide.region_4.6_spmd.clone.sunk | while | flops 2026634240 | bytes 48267516 | solution.py:97
  182.2 1.2 fusion.86
  183.4 2.7 exponential_divide_fusion.2
  188.4 1.7 fusion.89
  190.1 1.9 fusion.87
  192.0 1.3 fusion.86
  193.3 2.7 exponential_divide_fusion.2
  198.3 1.7 fusion.89
  200.0 1.9 fusion.87
  201.9 1.3 fusion.86
  203.2 2.7 exponential_divide_fusion.2
  208.2 1.7 fusion.89
  209.9 1.9 fusion.87
  211.8 7.4 %copy.115 = bf16[1536,2,128]{2,1,0:T(2,128)(2,1)} copy(bf16[1536,2,128]{2,0,1:T(8,128)(2,1)} %bitcast.172) | data formatting | bytes 1572864 | tf_op jit(solution)/shard_map/reshape | solution.py:102
  219.2 7.0 %all-to-all-start.5 = ((bf16[1536,2,128]{2,1,0:T(2,128)(2,1)}), bf16[1536,2,128]{2,1,0:T(2,128)(2,1)}, u32[]{:S(2)}, u32[]{:S(2)}) async-start(bf16[1536,2,128]{2,1,0:T(2,128)(2,1)} %copy.115), calls=%async_computation.5 | async-start | bytes 1572864 | tf_op jit(solution)/shard_map/all_to_all | solution.py:106
  226.2 2.0 copy.122
  228.2 11.7 %all-to-all-done.5 = bf16[1536,2,128]{2,1,0:T(2,128)(2,1)} async-done(((bf16[1536,2,128]{2,1,0:T(2,128)(2,1)}), bf16[1536,2,128]{2,1,0:T(2,128)(2,1)}, u32[]{:S(2)}, u32[]{:S(2)}) %all-to-all-start.5) | async-done | bytes 786464 | tf_op jit(solution)/shard_map/all_to_all | solution.py:106
  239.8 4.2 %all-to-all-start.7 = ((bf16[1536,2,128]{2,1,0:T(2,128)(2,1)}), bf16[1536,2,128]{2,1,0:T(2,128)(2,1)}, u32[]{:S(2)}, u32[]{:S(2)}) async-start(bf16[1536,2,128]{2,1,0:T(2,128)(2,1)} %copy.122), calls=%async_computation.7 | async-start | bytes 1572864 | tf_op jit(solution)/shard_map/all_to_all | solution.py:108
  244.7 7.3 %copy.119 = bf16[1536,2,128]{2,1,0:T(2,128)(2,1)} copy(bf16[1536,2,128]{2,0,1:T(8,128)(2,1)S(1)} %multiply_convert_fusion.1) | data formatting | bytes 1572864 | tf_op jit(solution)/shard_map/convert_element_type | solution.py:103
  252.0 4.7 %all-to-all-done.7 = bf16[1536,2,128]{2,1,0:T(2,128)(2,1)} async-done(((bf16[1536,2,128]{2,1,0:T(2,128)(2,1)}), bf16[1536,2,128]{2,1,0:T(2,128)(2,1)}, u32[]{:S(2)}, u32[]{:S(2)}) %all-to-all-start.7) | async-done | bytes 786464 | tf_op jit(solution)/shard_map/all_to_all | solution.py:108
  256.7 4.4 %all-to-all-start.6 = ((bf16[1536,2,128]{2,1,0:T(2,128)(2,1)}), bf16[1536,2,128]{2,1,0:T(2,128)(2,1)}, u32[]{:S(2)}, u32[]{:S(2)}) async-start(bf16[1536,2,128]{2,1,0:T(2,128)(2,1)} %copy.119), calls=%async_computation.6 | async-start | bytes 1572864 | tf_op jit(solution)/shard_map/all_to_all | solution.py:107
  261.1 1.2 copy.108
  263.2 1.5 reshape.89
  264.7 1.2 copy.116
  266.7 1.5 reshape.93
  268.2 1.2 copy.123
  269.5 1.7 copy.124
  271.2 3.3 reshape.95
  274.5 1.2 copy.120
  275.7 1.7 copy.121
  277.4 3.1 reshape.94
  280.6 65.6 %psum.7 = f32[]{:T(128)} all-reduce(f32[]{:T(128)} %get-tuple-element.281), channel_id=1, replica_groups=mesh['seq'=8,'batch'=16] {'seq','batch'}, use_global_device_ids=true, to_apply=%region_13.14 | all-reduce | flops 1 | bytes 8 | tf_op jit(solution)/shard_map/psum | solution.py:148
  348.2 47.8 %reduce-scatter.2.cloned.1.call-done = f32[16,768]{1,0:T(8,128)} async-done(((f32[2048,768]{1,0:T(8,128)}), f32[16,768]{1,0:T(8,128)}) %reduce-scatter.2.cloned.1.call-update) | async-done | bytes 49168 | tf_op jit(solution)/shard_map/reduce_scatter | solution.py:140
  397.0 1.5 subtract_divide_fusion
  (102 shorter events, 16.4 us)
Async XLA Ops:
  7.2 10.6 %copy-start.10 = (bf16[1,192,2048]{2,1,0:T(8,128)(2,1)S(1)}, bf16[1,192,2048]{2,1,0:T(8,128)(2,1)}, u32[]{:S(2)}) copy-start(bf16[1,192,2048]{2,1,0:T(8,128)(2,1)} %param.15) | copy-start | bytes 2359300
  9.6 26.1 %copy-start.11 = (bf16[1,192,2048]{2,1,0:T(8,128)(2,1)S(1)}, bf16[1,192,2048]{2,1,0:T(8,128)(2,1)}, u32[]{:S(2)}) copy-start(bf16[1,192,2048]{2,1,0:T(8,128)(2,1)} %param.16) | copy-start | bytes 2359300
  9.6 22.6 %all-to-all-start = ((bf16[192,16,128]{2,0,1:T(8,128)(2,1)}), bf16[192,16,128]{2,0,1:T(8,128)(2,1)S(1)}, u32[]{:S(2)}, u32[]{:S(2)}) async-start(bf16[192,16,128]{2,0,1:T(8,128)(2,1)} %copy.99), calls=%async_computation | async-start | bytes 1572864 | tf_op jit(solution)/shard_map/all_to_all | solution.py:43
  19.0 33.7 %copy-start.12 = (bf16[1,192,2048]{2,1,0:T(8,128)(2,1)S(1)}, bf16[1,192,2048]{2,1,0:T(8,128)(2,1)}, u32[]{:S(2)}) copy-start(bf16[1,192,2048]{2,1,0:T(8,128)(2,1)} %param.17) | copy-start | bytes 2359300
  32.2 17.0 %copy-start.5 = (bf16[192,16,128]{2,0,1:T(8,128)(2,1)}, bf16[192,16,128]{2,0,1:T(8,128)(2,1)S(1)}, u32[]{:S(2)}) copy-start(bf16[192,16,128]{2,0,1:T(8,128)(2,1)S(1)} %all-to-all-done) | copy-start | bytes 2359300
  32.2 17.0 %all-to-all-start.1 = ((bf16[192,16,128]{2,0,1:T(8,128)(2,1)}), bf16[192,16,128]{2,0,1:T(8,128)(2,1)S(1)}, u32[]{:S(2)}, u32[]{:S(2)}) async-start(bf16[192,16,128]{2,0,1:T(8,128)(2,1)} %copy.101), calls=%async_computation.1 | async-start | bytes 1572864 | tf_op jit(solution)/shard_map/all_to_all | solution.py:44
  35.9 18.1 %copy-start.14 = (bf16[16,768]{1,0:T(8,128)(2,1)S(1)}, bf16[16,768]{1,0:T(8,128)(2,1)}, u32[]{:S(2)}) copy-start(bf16[16,768]{1,0:T(8,128)(2,1)} %param.19) | copy-start | bytes 73732
  37.0 33.2 %copy-start.13 = (bf16[16,768]{1,0:T(8,128)(2,1)S(1)}, bf16[16,768]{1,0:T(8,128)(2,1)}, u32[]{:S(2)}) copy-start(bf16[16,768]{1,0:T(8,128)(2,1)} %param.18) | copy-start | bytes 73732
  37.0 34.8 %copy-start.19 = (s32[16]{0:T(128)S(1)}, s32[16]{0:T(128)}, u32[]{:S(2)}) copy-start(s32[16]{0:T(128)} %param.21) | copy-start | bytes 196
  49.2 16.1 %copy-start.6 = (bf16[192,16,128]{2,0,1:T(8,128)(2,1)}, bf16[192,16,128]{2,0,1:T(8,128)(2,1)S(1)}, u32[]{:S(2)}) copy-start(bf16[192,16,128]{2,0,1:T(8,128)(2,1)S(1)} %all-to-all-done.1) | copy-start | bytes 2359300
  49.2 16.1 %all-to-all-start.2 = ((bf16[192,16,128]{2,0,1:T(8,128)(2,1)}), bf16[192,16,128]{2,0,1:T(8,128)(2,1)S(1)}, u32[]{:S(2)}, u32[]{:S(2)}) async-start(bf16[192,16,128]{2,0,1:T(8,128)(2,1)} %copy.103), calls=%async_computation.2 | async-start | bytes 1572864 | tf_op jit(solution)/shard_map/all_to_all | solution.py:45
  65.3 5.2 %copy-start.8 = (bf16[192,16,128]{2,0,1:T(8,128)(2,1)}, bf16[192,16,128]{2,0,1:T(8,128)(2,1)S(1)}, u32[]{:S(2)}) copy-start(bf16[192,16,128]{2,0,1:T(8,128)(2,1)S(1)} %all-to-all-done.2) | copy-start | bytes 2359300
  65.3 76.9 %all-to-all-start.4 = ((bf16[192,16,128]{2,0,1:T(8,128)(2,1)}), bf16[192,16,128]{2,0,1:T(8,128)(2,1)}, u32[]{:S(2)}, u32[]{:S(2)}) async-start(bf16[192,16,128]{2,0,1:T(8,128)(2,1)} %copy.110), calls=%async_computation.4 | async-start | bytes 1572864 | tf_op jit(solution)/shard_map/all_to_all | solution.py:76
  69.5 105.4 %all-gather.2.cloned.1.call-start = ((), (), s32[]{:S(2)}) async-start(), calls=%async_computation.9 | async-start | bytes 3170304 | tf_op jit(solution)/shard_map/all_gather | solution.py:124
  69.5 72.7 %copy-start.17 = (f32[16]{0:T(128)}, f32[16]{0:T(128)S(1)}, u32[]{:S(2)}) copy-start(f32[16]{0:T(128)S(1)} %add_sqrt_fusion) | copy-start | bytes 196
  138.1 2.2 copy-start.7
  138.1 3.2 copy-start.9
  146.6 1.2 copy-start.1
  152.4 1.2 copy-start.1
  158.2 1.2 copy-start.1
  161.7 13.2 %copy-start.16 = (s32[16]{0:T(128)S(1)}, s32[16]{0:T(128)}, u32[]{:S(2)}) copy-start(s32[16]{0:T(128)} %param.20) | copy-start | bytes 196
  170.1 49.1 %all-to-all-start.3 = ((bf16[1536,2,128]{2,1,0:T(2,128)(2,1)}), bf16[1536,2,128]{2,1,0:T(2,128)(2,1)}, u32[]{:S(2)}, u32[]{:S(2)}) async-start(bf16[1536,2,128]{2,1,0:T(2,128)(2,1)} %copy.107), calls=%async_computation.3 | async-start | bytes 1572864 | tf_op jit(solution)/shard_map/all_to_all | solution.py:75
  174.6 221.4 %reduce-scatter.2.cloned.1.call-start = ((), (), s32[]{:S(2)}) async-start(), calls=%async_computation.10 | async-start | bytes 6340608 | tf_op jit(solution)/shard_map/reduce_scatter | solution.py:140
  183.4 2.7 copy-start.3
  186.1 1.1 copy-start.2
  187.3 1.1 copy-start
  193.3 2.7 copy-start.3
  196.0 1.1 copy-start.2
  197.1 1.1 copy-start
  203.2 2.7 copy-start.3
  205.9 1.1 copy-start.2
  207.0 1.1 copy-start
  219.2 20.6 %all-to-all-start.5 = ((bf16[1536,2,128]{2,1,0:T(2,128)(2,1)}), bf16[1536,2,128]{2,1,0:T(2,128)(2,1)}, u32[]{:S(2)}, u32[]{:S(2)}) async-start(bf16[1536,2,128]{2,1,0:T(2,128)(2,1)} %copy.115), calls=%async_computation.5 | async-start | bytes 1572864 | tf_op jit(solution)/shard_map/all_to_all | solution.py:106
  239.8 16.8 %all-to-all-start.7 = ((bf16[1536,2,128]{2,1,0:T(2,128)(2,1)}), bf16[1536,2,128]{2,1,0:T(2,128)(2,1)}, u32[]{:S(2)}, u32[]{:S(2)}) async-start(bf16[1536,2,128]{2,1,0:T(2,128)(2,1)} %copy.122), calls=%async_computation.7 | async-start | bytes 1572864 | tf_op jit(solution)/shard_map/all_to_all | solution.py:108
  256.7 17.8 %all-to-all-start.6 = ((bf16[1536,2,128]{2,1,0:T(2,128)(2,1)}), bf16[1536,2,128]{2,1,0:T(2,128)(2,1)}, u32[]{:S(2)}, u32[]{:S(2)}) async-start(bf16[1536,2,128]{2,1,0:T(2,128)(2,1)} %copy.119), calls=%async_computation.6 | async-start | bytes 1572864 | tf_op jit(solution)/shard_map/all_to_all | solution.py:107
  271.2 75.7 %copy-start.4 = (bf16[2048,768]{1,0:T(8,128)(2,1)S(1)}, bf16[2048,768]{1,0:T(8,128)(2,1)}, u32[]{:S(2)}) copy-start(bf16[2048,768]{1,0:T(8,128)(2,1)} %all-gather.2.cloned.1.call-done) | copy-start | bytes 9437188
  275.7 120.3 %copy-start.15 = (bf16[16,768]{1,0:T(8,128)(2,1)S(1)}, bf16[16,768]{1,0:T(8,128)(2,1)}, u32[]{:S(2)}) copy-start(bf16[16,768]{1,0:T(8,128)(2,1)} %param.19) | copy-start | bytes 73732
  275.7 120.3 %copy-start.18 = (f32[16]{0:T(128)S(1)}, f32[16]{0:T(128)}, u32[]{:S(2)}) copy-start(f32[16]{0:T(128)} %copy-done.17) | copy-start | bytes 196
Sparse Core Ops, SparseCore 0:
  74.0 67.7 all-gather.1
  182.3 213.6 reduce-scatter.1
where the time goes:
time: 408 us; the launch traced here: 406 us
  blocking collectives  132 us (32%)
  waiting for transfers between devices  101 us (25%)
  local copies, waits for them, and re-layouts  58.9 us (14%)
  matrix products  46.1 us (11%)
  starting transfers between devices  39.9 us (10%)
  between operations  17.5 us (4%)
  other arithmetic  11.6 us (3%)
    unnamed x1, blocking collectives  66 us
    psum x1, blocking collectives, body(): loss_sum = lax.psum(total, ('seq', 'batch'))  65.6 us
    reduce_scatter x1, waiting for transfers between devices, body(): lax.psum_scatter(lax.dot_general(pair_grad, clip_b, (((0,), (0,)), ((), (...  47.8 us
    dot_general x6, matrix products, block_scores(): jnp.einsum('qhd,khd->hqk', q_block, k_heads, preferred_element_type=jnp.f...  14.9 us
    all_to_all x1, waiting for transfers between devices, body(): lax.all_to_all(split_heads(queries), 'seq', split_axis=1, concat_axis=0,...  13.1 us
    all_to_all x1, waiting for transfers between devices, body(): lax.all_to_all(split_heads(key_vectors), 'seq', split_axis=1, concat_axis...  12.2 us
    all_to_all x1, waiting for transfers between devices, body(): lax.all_to_all(dq_heads, 'seq', split_axis=0, concat_axis=1, tiled=True)  11.7 us
    all_to_all x1, waiting for transfers between devices, body(): lax.all_to_all(split_heads(value_vectors), 'seq', split_axis=1, concat_ax...  11.1 us
  transfers between devices with their start and end apart: 10, of which 6 were waited for; matrix products, arithmetic and copies ran while one was open for 27% of the time, Pallas kernels for 0%

commit v1 on v0

v1 whole, which is shorter than its diff:
```python
import functools
import math

import jax
import jax.numpy as jnp
from jax import lax
from jax.experimental import pallas as pl
from jax.experimental.pallas import tpu as pltpu
from jax.sharding import PartitionSpec as P

MESH = pl.DeviceIdType.MESH
F32 = jnp.float32
BF16 = jnp.bfloat16

HD = 128
SEQ = 8
BATCH = 16
NZ = 4
NY = 4
NXC = 8
HEADS_HERE = 2
BLOCK_Q = 512

INV_ROOT = 1.0 / math.sqrt(HD)
EXP2_SCALE = INV_ROOT * math.log2(math.e)


def nt(a, b):
    return lax.dot_general(a, b, (((1,), (1,)), ((), ())), preferred_element_type=F32)


def nn(a, b):
    return lax.dot_general(a, b, (((1,), (0,)), ((), ())), preferred_element_type=F32)


def tn(a, b):
    return lax.dot_general(a, b, (((0,), (0,)), ((), ())), preferred_element_type=F32)


def aligned(index, size):
    return pl.ds(pl.multiple_of(index * size, size), size)


def unit_rows(raw):
    rawf = raw.astype(F32)
    norm = jnp.sqrt(jnp.sum(rawf * rawf, axis=1, keepdims=True) + 1e-06)
    return (rawf / norm, norm)


def raw_grad(raw, direction):
    unit, norm = unit_rows(raw)
    return (direction - unit * jnp.sum(unit * direction, axis=1, keepdims=True)) / norm


def wait_for(ref, sem):
    pltpu.make_async_copy(ref, ref, sem).wait()


def column_of_ids(ids_ref, rows):
    row = lax.broadcasted_iota(jnp.int32, (rows, HD), 0)
    column = jnp.zeros((rows, HD), jnp.int32)
    for i in range(rows):
        column = jnp.where(row == i, ids_ref[i], column)
    return column


def kernel(
    q_in, k_in, v_in, d_in, clip_raw, text_raw, clip_ids, text_ids, scale_ref, bias_ref,
    o_out, dq_out, dk_out, dv_out, grad_clip, grad_text, loss_out,
    land, res, dk_sum, dv_sum,
    clip_y, clip_y_ids, clip_x, clip_x_ids, text_z, text_z_ids,
    dx_send, dx_recv, dy_send, dy_recv, dt_send, dt_recv, loss_send, loss_recv,
    in_send, in_recv, in_local, out_send, out_recv, out_local, small_send, small_recv,
):
    tokens = q_in.shape[1]
    rows = clip_raw.shape[0]
    full = tokens * SEQ
    s = lax.axis_index("seq")
    b = lax.axis_index("batch")
    z, y_hi = s // 2, s % 2
    y_lo, xc = b // NXC, b % NXC
    y = y_hi * 2 + y_lo

    def seq_peer(k):
        return (lax.rem(s + k, SEQ), b)

    def xc_peer(k):
        return (s, y_lo * NXC + lax.rem(xc + k, NXC))

    def y_peer(k):
        other = lax.rem(y + k, NY)
        return (z * 2 + other // 2, (other % 2) * NXC + xc)

    def z_peer(k):
        return (lax.rem(z + k, NZ) * 2 + y_hi, b)

    barrier = pltpu.get_barrier_semaphore()

    def greet(peer):
        pl.semaphore_signal(barrier, inc=1, device_id=peer, device_id_type=MESH)

    for k in range(1, SEQ):
        greet(seq_peer(k))
    for k in range(1, NXC):
        greet(xc_peer(k))
    greet(y_peer(1))
    greet(y_peer(3))

    clip_y[aligned(y, rows), :] = unit_rows(clip_raw[...])[0].astype(BF16)
    text_z[aligned(z, rows), :] = unit_rows(text_raw[...])[0].astype(BF16)
    clip_y_ids[aligned(y, rows), :] = column_of_ids(clip_ids, rows)
    text_z_ids[aligned(z, rows), :] = column_of_ids(text_ids, rows)

    pl.semaphore_wait(barrier, SEQ - 1 + NXC - 1 + 2)

    def send(src, dst, index, peer):
        pltpu.make_async_remote_copy(
            src_ref=src, dst_ref=dst, send_sem=small_send.at[index], recv_sem=small_recv.at[index],
            device_id=peer, device_id_type=MESH,
        ).start()

    for k in range(1, NY):
        mine = aligned(y, rows)
        send(clip_y.at[mine], clip_y.at[mine], 0, y_peer(k))
        send(clip_y_ids.at[mine], clip_y_ids.at[mine], 1, y_peer(k))
    for k in range(1, NZ):
        mine = aligned(z, rows)
        send(text_z.at[mine], text_z.at[mine], 2, z_peer(k))
        send(text_z_ids.at[mine], text_z_ids.at[mine], 3, z_peer(k))

    ins = (k_in, q_in, v_in, d_in)

    def send_head(h):
        for a, ref in enumerate(ins):
            mine = aligned(s, tokens)
            pltpu.make_async_copy(
                ref.at[0, :, aligned(s * HEADS_HERE + h, HD)], land.at[h, a, mine], in_local.at[h, a]
            ).start()

            def to_peer(k, carry):
                peer = seq_peer(k)
                pltpu.make_async_remote_copy(
                    src_ref=ref.at[0, :, aligned(peer[0] * HEADS_HERE + h, HD)],
                    dst_ref=land.at[h, a, mine],
                    send_sem=in_send.at[h, a], recv_sem=in_recv.at[h, a],
                    device_id=peer, device_id_type=MESH,
                ).start()
                return carry

            lax.fori_loop(1, SEQ, to_peer, 0)

    others = full - tokens

    def wait_sent(h):
        for a in range(4):
            wait_for(land.at[h, a, pl.ds(0, others)], in_send.at[h, a])

    def wait_head(h, a):
        wait_for(land.at[h, a, pl.ds(0, others)], in_recv.at[h, a])
        wait_for(land.at[h, a, pl.ds(0, tokens)], in_local.at[h, a])

    send_head(0)

    wait_for(clip_y.at[pl.ds(0, 3 * rows)], small_recv.at[0])
    wait_for(clip_y_ids.at[pl.ds(0, 3 * rows)], small_recv.at[1])
    group = NY * rows
    for k in range(1, NXC):
        send(clip_y, clip_x.at[aligned(xc, group)], 4, xc_peer(k))
        send(clip_y_ids, clip_x_ids.at[aligned(xc, group)], 5, xc_peer(k))
    clip_x[aligned(xc, group), :] = clip_y[...]
    clip_x_ids[aligned(xc, group), :] = clip_y_ids[...]

    wait_sent(0)
    send_head(1)

    wait_for(text_z.at[pl.ds(0, 3 * rows)], small_recv.at[2])
    wait_for(text_z_ids.at[pl.ds(0, 3 * rows)], small_recv.at[3])
    wait_for(clip_x.at[pl.ds(0, 7 * group)], small_recv.at[4])
    wait_for(clip_x_ids.at[pl.ds(0, 7 * group)], small_recv.at[5])
    scale = scale_ref[0]
    offset = bias_ref[0]
    clip_all = clip_x[...]
    text_all = text_z[...]
    texts = NZ * rows
    logits = scale * nt(clip_all, text_all) + offset
    text_row = jnp.transpose(text_z_ids[...].astype(F32))[0:1, :]
    clip_column = clip_x_ids[...].astype(F32)[:, 0:texts]
    sign = jnp.where(clip_column == text_row, F32(1.0), F32(-1.0))
    turned = -sign * logits
    small = jnp.exp(-jnp.abs(turned))
    sigmoid = jnp.where(turned >= 0, F32(1.0), small) / (1.0 + small)
    loss_here = jnp.sum(jnp.maximum(turned, 0.0) + jnp.log1p(small))
    pair_grad = (scale * -sign * sigmoid).astype(BF16)
    text_part = tn(pair_grad, clip_all)
    for j in range(NZ):
        dt_send[j] = text_part[j * rows : (j + 1) * rows]
    clip_part = nn(pair_grad, text_all)
    for j in range(NXC):
        dx_send[j, 0:group] = clip_part[j * group : (j + 1) * group]
        dx_send[j, group : group + 8] = jnp.full((8, clip_part.shape[1]), loss_here, F32)
    for k in range(1, NXC):
        send(dx_send.at[lax.rem(xc + k, NXC)], dx_recv.at[xc], 6, xc_peer(k))
    for k in range(1, NZ):
        send(dt_send.at[lax.rem(z + k, NZ)], dt_recv.at[z], 7, z_peer(k))
    dx_recv[xc] = dx_send[xc]
    dt_recv[z] = dt_send[z]

    def attend(h):
        k_all, q_all, v_all, d_all = (land.at[h, a] for a in range(4))
        for a in range(4):
            wait_head(h, a)
        dk_sum[...] = jnp.zeros_like(dk_sum)
        dv_sum[...] = jnp.zeros_like(dv_sum)

        def step(i, carry):
            r = aligned(i, BLOCK_Q)
            q = q_all[r, :]
            d = d_all[r, :]
            raw_scores = nt(q, k_all[...])
            top = jnp.max(raw_scores, axis=1, keepdims=True)
            expo = jnp.exp2(raw_scores * EXP2_SCALE - top * EXP2_SCALE)
            total = jnp.sum(expo, axis=1, keepdims=True)
            probs = expo * (1.0 / total)
            probs_b = probs.astype(BF16)
            out = nn(probs_b, v_all[...]).astype(BF16)
            res[h, 0, r, :] = out
            dv_sum[...] += tn(probs_b, d)
            dprobs = nt(d, v_all[...])
            delta = jnp.sum(d.astype(F32) * out.astype(F32), axis=1, keepdims=True)
            dscores = (probs * (dprobs - delta)).astype(BF16)
            res[h, 1, r, :] = (nn(dscores, k_all[...]) * INV_ROOT).astype(BF16)
            dk_sum[...] += tn(dscores, q)
            return carry

        lax.fori_loop(0, full // BLOCK_Q, step, 0)
        res[h, 2] = (dk_sum[...] * INV_ROOT).astype(BF16)
        res[h, 3] = dv_sum[...].astype(BF16)

    outs = (o_out, dq_out, dk_out, dv_out)

    def return_head(h):
        for a, ref in enumerate(outs):
            columns = aligned(s * HEADS_HERE + h, HD)
            pltpu.make_async_copy(
                res.at[h, a, aligned(s, tokens)], ref.at[0, :, columns], out_local.at[a]
            ).start()

            def to_peer(k, carry):
                peer = seq_peer(k)
                pltpu.make_async_remote_copy(
                    src_ref=res.at[h, a, aligned(peer[0], tokens)],
                    dst_ref=ref.at[0, :, columns],
                    send_sem=out_send.at[a], recv_sem=out_recv.at[a],
                    device_id=peer, device_id_type=MESH,
                ).start()
                return carry

            lax.fori_loop(1, SEQ, to_peer, 0)

    attend(0)
    return_head(0)

    wait_for(dx_recv.at[pl.ds(0, NXC - 1)], small_recv.at[6])
    clip_sum = dx_recv[0]
    for j in range(1, NXC):
        clip_sum = clip_sum + dx_recv[j]
    for j in range(NY):
        dy_send[j, 0:rows] = clip_sum[j * rows : (j + 1) * rows]
        dy_send[j, rows : rows + 8] = clip_sum[group : group + 8]
    for k in range(1, NY):
        send(dy_send.at[lax.rem(y + k, NY)], dy_recv.at[y], 8, y_peer(k))
    dy_recv[y] = dy_send[y]

    attend(1)
    return_head(1)

    wait_for(dy_recv.at[pl.ds(0, NY - 1)], small_recv.at[8])
    clip_sum = dy_recv[0]
    for j in range(1, NY):
        clip_sum = clip_sum + dy_recv[j]
    loss_send[...] = clip_sum[rows : rows + 8, 0:HD]
    for k in range(1, NZ):
        send(loss_send, loss_recv.at[z], 9, z_peer(k))
    loss_recv[z] = loss_send[...]
    grad_clip[...] = raw_grad(clip_raw[...], clip_sum[0:rows])

    wait_for(dt_recv.at[pl.ds(0, NZ - 1)], small_recv.at[7])
    text_sum = dt_recv[0]
    for j in range(1, NZ):
        text_sum = text_sum + dt_recv[j]
    grad_text[...] = raw_grad(text_raw[...], text_sum)

    wait_for(loss_recv.at[pl.ds(0, NZ - 1)], small_recv.at[9])
    loss_sum = loss_recv[0]
    for j in range(1, NZ):
        loss_sum = loss_sum + loss_recv[j]
    loss_out[0] = loss_sum[0, 0] / (rows * SEQ * BATCH)

    for index, ref in (
        (0, clip_y.at[pl.ds(0, 3 * rows)]),
        (1, clip_y_ids.at[pl.ds(0, 3 * rows)]),
        (2, text_z.at[pl.ds(0, 3 * rows)]),
        (3, text_z_ids.at[pl.ds(0, 3 * rows)]),
        (4, clip_x.at[pl.ds(0, 7 * group)]),
        (5, clip_x_ids.at[pl.ds(0, 7 * group)]),
        (6, dx_recv.at[pl.ds(0, NXC - 1)]),
        (7, dt_recv.at[pl.ds(0, NZ - 1)]),
        (8, dy_recv.at[pl.ds(0, NY - 1)]),
        (9, loss_recv.at[pl.ds(0, NZ - 1)]),
    ):
        wait_for(ref, small_send.at[index])
    wait_sent(1)
    remote = HEADS_HERE * (SEQ - 1) * HD
    for a, ref in enumerate(outs):
        wait_for(ref.at[0, :, pl.ds(0, HEADS_HERE * HD)], out_local.at[a])
        wait_for(ref.at[0, :, pl.ds(0, remote)], out_send.at[a])
        wait_for(ref.at[0, :, pl.ds(0, remote)], out_recv.at[a])


def body(queries, key_vectors, value_vectors, cotangent, clip_raw, text_raw, clip_video, text_video, logit_scale, logit_bias):
    tokens = queries.shape[1]
    full = tokens * SEQ
    rows, width = clip_raw.shape
    in_hbm = pl.BlockSpec(memory_space=pl.ANY)
    in_vmem = pl.BlockSpec(memory_space=pltpu.VMEM)
    in_smem = pl.BlockSpec(memory_space=pltpu.SMEM)
    group = NY * rows
    dma = pltpu.SemaphoreType.DMA
    return pl.pallas_call(
        kernel,
        out_shape=(
            *[jax.ShapeDtypeStruct(queries.shape, BF16)] * 4,
            jax.ShapeDtypeStruct((rows, width), F32),
            jax.ShapeDtypeStruct((rows, width), F32),
            jax.ShapeDtypeStruct((1,), F32),
        ),
        in_specs=[in_hbm] * 4 + [in_vmem] * 2 + [in_smem] * 4,
        out_specs=(*[in_hbm] * 4, in_vmem, in_vmem, in_smem),
        scratch_shapes=[
            pltpu.VMEM((HEADS_HERE, 4, full, HD), BF16),
            pltpu.VMEM((HEADS_HERE, 4, full, HD), BF16),
            pltpu.VMEM((full, HD), F32),
            pltpu.VMEM((full, HD), F32),
            pltpu.VMEM((group, width), BF16),
            pltpu.VMEM((group, HD), jnp.int32),
            pltpu.VMEM((NXC * group, width), BF16),
            pltpu.VMEM((NXC * group, HD), jnp.int32),
            pltpu.VMEM((NZ * rows, width), BF16),
            pltpu.VMEM((NZ * rows, HD), jnp.int32),
            pltpu.VMEM((NXC, group + 8, width), F32),
            pltpu.VMEM((NXC, group + 8, width), F32),
            pltpu.VMEM((NY, rows + 8, width), F32),
            pltpu.VMEM((NY, rows + 8, width), F32),
            pltpu.VMEM((NZ, rows, width), F32),
            pltpu.VMEM((NZ, rows, width), F32),
            pltpu.VMEM((8, HD), F32),
            pltpu.VMEM((NZ, 8, HD), F32),
            dma((HEADS_HERE, 4)),
            dma((HEADS_HERE, 4)),
            dma((HEADS_HERE, 4)),
            dma((4,)),
            dma((4,)),
            dma((4,)),
            dma((10,)),
            dma((10,)),
        ],
        compiler_params=pltpu.CompilerParams(
            collective_id=0, has_side_effects=True, vmem_limit_bytes=56 * 2**20
        ),
        cost_estimate=pl.CostEstimate(
            flops=HEADS_HERE * 12 * full * full * HD, bytes_accessed=8 * full * HD * 2, transcendentals=HEADS_HERE * full * full
        ),
        name="tower",
    )(queries, key_vectors, value_vectors, cotangent, clip_raw, text_raw, clip_video, text_video, logit_scale, logit_bias)


def solution(mesh):
    tokens = P("batch", "seq", None)
    embeddings = P(("seq", "batch"), None)
    ids = P(("seq", "batch"))
    return jax.shard_map(
        body,
        mesh=mesh,
        in_specs=(tokens,) * 4 + (embeddings,) * 2 + (ids,) * 2 + (P(), P()),
        out_specs=(tokens,) * 4 + (embeddings,) * 2 + (P(),),
        check_vma=False,
    )
```

time: 408 us -> 136 us (0.33)
  the two profiles are of different devices: /device:TPU:0 before, /device:TPU:17 now
where the time goes in v1:
time: 136 us
  Pallas kernels  125 us (92%)
  local copies, waits for them, and re-layouts  7.32 us (5%)
  between operations  3.71 us (3%)
    pallas_call x1, Pallas kernels, body(): pl.pallas_call(kernel, out_shape=(*[jax.ShapeDtypeStruct(queries.shape, B...  125 us
    unnamed x16, local copies, waits for them, and re-layouts  7.32 us

profile of v1, /device:TPU:17, one launch (start us, length us, event | category | flops | bytes accessed | tf_op | source)
XLA Modules:
  0.0 136.0 jit_solution(16047096998472540693)
XLA Ops:
  1.9 125.0 %tower.1 = (bf16[1,192,2048]{2,1,0:T(8,128)(2,1)}, bf16[1,192,2048]{2,1,0:T(8,128)(2,1)}, bf16[1,192,2048]{2,1,0:T(8,128)(2,1)}, bf16[1,192,2048]{2,1,0:T(8,128)...) custom-call(bf16[1,192,2048]{2,1,0:T(8,128)(2,1)} %q_in.1, bf16[1,192,2048]{2,1,0:T(8,128)(2,1)} %k_in.1, ...), custom_call_target="tpu_custom_call" | custom-call | flops 7247757312 | bytes 3145728 | tf_op jit(solution)/shard_map/tower/pallas_call | solution.py:329
  126.9 0.0 copy-start.2
  126.9 2.2 %copy.26 = bf16[1,192,2048]{2,1,0:T(8,128)(2,1)} copy(bf16[1,192,2048]{2,1,0:T(8,128)(2,1)} %get-tuple-element.14) | data formatting | bytes 1572864
  129.1 0.0 copy-done.2
  129.1 0.0 copy-start.1
  129.1 0.9 copy.27
  129.9 0.5 copy-done.1
  130.5 0.0 copy-start
  130.5 0.9 copy.28
  131.4 0.5 copy-done
  131.9 0.0 copy-start.4
  131.9 0.9 copy.29
  132.8 0.0 copy-done.4
  132.8 0.0 copy-start.3
  132.8 0.6 copy.30
  133.4 0.2 copy-done.3
  133.6 0.6 copy.31
Async XLA Ops:
  126.9 2.2 %copy-start.2 = (bf16[1,192,2048]{2,1,0:T(8,128)(2,1)S(1)}, bf16[1,192,2048]{2,1,0:T(8,128)(2,1)}, u32[]{:S(2)}) copy-start(bf16[1,192,2048]{2,1,0:T(8,128)(2,1)} %get-tuple-element.15) | copy-start | bytes 2359300
  129.1 1.4 %copy-start.1 = (bf16[1,192,2048]{2,1,0:T(8,128)(2,1)S(1)}, bf16[1,192,2048]{2,1,0:T(8,128)(2,1)}, u32[]{:S(2)}) copy-start(bf16[1,192,2048]{2,1,0:T(8,128)(2,1)} %get-tuple-element.16) | copy-start | bytes 2359300
  130.5 1.4 %copy-start = (bf16[1,192,2048]{2,1,0:T(8,128)(2,1)S(1)}, bf16[1,192,2048]{2,1,0:T(8,128)(2,1)}, u32[]{:S(2)}) copy-start(bf16[1,192,2048]{2,1,0:T(8,128)(2,1)} %get-tuple-element.17) | copy-start | bytes 2359300
  131.9 0.9 copy-start.4
  132.8 0.8 copy-start.3

commit v2 on v1

--- a/solution.py
+++ b/solution.py
@@ -17,9 +17,11 @@
 BATCH = 16
 NZ = 4
 NY = 4
-NXC = 8
+NX = 4
+NC = 2
 HEADS_HERE = 2
 BLOCK_Q = 512
+PIECES = 2
 
 INV_ROOT = 1.0 / math.sqrt(HD)
 EXP2_SCALE = INV_ROOT * math.log2(math.e)
@@ -68,8 +70,8 @@
     q_in, k_in, v_in, d_in, clip_raw, text_raw, clip_ids, text_ids, scale_ref, bias_ref,
     o_out, dq_out, dk_out, dv_out, grad_clip, grad_text, loss_out,
     land, res, dk_sum, dv_sum,
-    clip_y, clip_y_ids, clip_x, clip_x_ids, text_z, text_z_ids,
-    dx_send, dx_recv, dy_send, dy_recv, dt_send, dt_recv, loss_send, loss_recv,
+    clip_y, clip_y_ids, clip_x, clip_x_ids, text_z, text_z_ids, text_c, text_c_ids,
+    dc_send, dc_recv, dx_send, dx_recv, near_send, near_recv, far_send, far_recv, loss_y, dt_send, dt_recv, loss_send, loss_recv,
     in_send, in_recv, in_local, out_send, out_recv, out_local, small_send, small_recv,
 ):
     tokens = q_in.shape[1]
@@ -78,18 +80,22 @@
     s = lax.axis_index("seq")
     b = lax.axis_index("batch")
     z, y_hi = s // 2, s % 2
-    y_lo, xc = b // NXC, b % NXC
+    y_lo, x, c = b // (NX * NC), (b // NC) % NX, b % NC
     y = y_hi * 2 + y_lo
 
     def seq_peer(k):
         return (lax.rem(s + k, SEQ), b)
 
-    def xc_peer(k):
-        return (s, y_lo * NXC + lax.rem(xc + k, NXC))
+    def x_peer(k):
+        return (s, (y_lo * NX + lax.rem(x + k, NX)) * NC + c)
 
     def y_peer(k):
         other = lax.rem(y + k, NY)
-        return (z * 2 + other // 2, (other % 2) * NXC + xc)
+        return (z * 2 + other // 2, ((other % 2) * NX + x) * NC + c)
+
+    y_near = (s, b + (1 - 2 * y_lo) * NX * NC)
+    y_far = (s + 1 - 2 * y_hi, b)
+    c_peer = (s, b + 1 - 2 * c)
 
     def z_peer(k):
         return (lax.rem(z + k, NZ) * 2 + y_hi, b)
@@ -101,8 +107,9 @@
 
     for k in range(1, SEQ):
         greet(seq_peer(k))
-    for k in range(1, NXC):
-        greet(xc_peer(k))
+    for k in range(1, NX):
+        greet(x_peer(k))
+    greet(c_peer)
     greet(y_peer(1))
     greet(y_peer(3))
 
@@ -111,7 +118,7 @@
     clip_y_ids[aligned(y, rows), :] = column_of_ids(clip_ids, rows)
     text_z_ids[aligned(z, rows), :] = column_of_ids(text_ids, rows)
 
-    pl.semaphore_wait(barrier, SEQ - 1 + NXC - 1 + 2)
+    pl.semaphore_wait(barrier, SEQ - 1 + NX - 1 + 3)
 
     def send(src, dst, index, peer):
         pltpu.make_async_remote_copy(
@@ -159,51 +166,63 @@
         wait_for(land.at[h, a, pl.ds(0, others)], in_recv.at[h, a])
         wait_for(land.at[h, a, pl.ds(0, tokens)], in_local.at[h, a])
 
-    send_head(0)
-
     wait_for(clip_y.at[pl.ds(0, 3 * rows)], small_recv.at[0])
     wait_for(clip_y_ids.at[pl.ds(0, 3 * rows)], small_recv.at[1])
-    group = NY * rows
-    for k in range(1, NXC):
-        send(clip_y, clip_x.at[aligned(xc, group)], 4, xc_peer(k))
-        send(clip_y_ids, clip_x_ids.at[aligned(xc, group)], 5, xc_peer(k))
-    clip_x[aligned(xc, group), :] = clip_y[...]
-    clip_x_ids[aligned(xc, group), :] = clip_y_ids[...]
-
-    wait_sent(0)
-    send_head(1)
-
     wait_for(text_z.at[pl.ds(0, 3 * rows)], small_recv.at[2])
     wait_for(text_z_ids.at[pl.ds(0, 3 * rows)], small_recv.at[3])
-    wait_for(clip_x.at[pl.ds(0, 7 * group)], small_recv.at[4])
-    wait_for(clip_x_ids.at[pl.ds(0, 7 * group)], small_recv.at[5])
+
+    send_head(0)
+
+    group = NY * rows
+    for k in range(1, NX):
+        send(clip_y, clip_x.at[aligned(x, group)], 4, x_peer(k))
+        send(clip_y_ids, clip_x_ids.at[aligned(x, group)], 5, x_peer(k))
+    clip_x[aligned(x, group), :] = clip_y[...]
+    clip_x_ids[aligned(x, group), :] = clip_y_ids[...]
+    send(text_z, text_c.at[aligned(c, group)], 6, c_peer)
+    send(text_z_ids, text_c_ids.at[aligned(c, group)], 7, c_peer)
+    text_c[aligned(c, group), :] = text_z[...]
+    text_c_ids[aligned(c, group), :] = text_z_ids[...]
+
+    wait_for(text_c.at[pl.ds(0, group)], small_recv.at[6])
+    wait_for(text_c_ids.at[pl.ds(0, group)], small_recv.at[7])
+    wait_for(clip_x.at[pl.ds(0, 3 * group)], small_recv.at[4])
+    wait_for(clip_x_ids.at[pl.ds(0, 3 * group)], small_recv.at[5])
     scale = scale_ref[0]
     offset = bias_ref[0]
     clip_all = clip_x[...]
-    text_all = text_z[...]
-    texts = NZ * rows
+    text_all = text_c[...]
     logits = scale * nt(clip_all, text_all) + offset
-    text_row = jnp.transpose(text_z_ids[...].astype(F32))[0:1, :]
-    clip_column = clip_x_ids[...].astype(F32)[:, 0:texts]
-    sign = jnp.where(clip_column == text_row, F32(1.0), F32(-1.0))
+    text_row = jnp.transpose(text_c_ids[...].astype(F32))[0:1, :]
+    sign = jnp.where(clip_x_ids[...].astype(F32) == text_row, F32(1.0), F32(-1.0))
     turned = -sign * logits
     small = jnp.exp(-jnp.abs(turned))
     sigmoid = jnp.where(turned >= 0, F32(1.0), small) / (1.0 + small)
     loss_here = jnp.sum(jnp.maximum(turned, 0.0) + jnp.log1p(small))
     pair_grad = (scale * -sign * sigmoid).astype(BF16)
     text_part = tn(pair_grad, clip_all)
+    for j in range(NC):
+        dc_send[j, 0:group] = text_part[j * group : (j + 1) * group]
+        dc_send[j, group : group + 8] = jnp.full((8, text_part.shape[1]), loss_here, F32)
+    send(dc_send.at[1 - c], dc_recv, 8, c_peer)
+    clip_part = nn(pair_grad, text_all)
+    for j in range(NX):
+        dx_send[j, 0:group] = clip_part[j * group : (j + 1) * group]
+    wait_for(dc_recv, small_recv.at[8])
+    text_sum = dc_send[c] + dc_recv[...]
     for j in range(NZ):
-        dt_send[j] = text_part[j * rows : (j + 1) * rows]
-    clip_part = nn(pair_grad, text_all)
-    for j in range(NXC):
-        dx_send[j, 0:group] = clip_part[j * group : (j + 1) * group]
-        dx_send[j, group : group + 8] = jnp.full((8, clip_part.shape[1]), loss_here, F32)
-    for k in range(1, NXC):
-        send(dx_send.at[lax.rem(xc + k, NXC)], dx_recv.at[xc], 6, xc_peer(k))
+        dt_send[j] = text_sum[j * rows : (j + 1) * rows]
+    for j in range(NX):
+        dx_send[j, group : group + 8] = text_sum[group : group + 8]
+    for k in range(1, NX):
+        send(dx_send.at[lax.rem(x + k, NX)], dx_recv.at[x], 9, x_peer(k))
     for k in range(1, NZ):
-        send(dt_send.at[lax.rem(z + k, NZ)], dt_recv.at[z], 7, z_peer(k))
-    dx_recv[xc] = dx_send[xc]
+        send(dt_send.at[lax.rem(z + k, NZ)], dt_recv.at[z], 10, z_peer(k))
+    dx_recv[x] = dx_send[x]
     dt_recv[z] = dt_send[z]
+
+    wait_sent(0)
+    send_head(1)
 
     def attend(h):
         k_all, q_all, v_all, d_all = (land.at[h, a] for a in range(4))
@@ -260,53 +279,68 @@
     attend(0)
     return_head(0)
 
-    wait_for(dx_recv.at[pl.ds(0, NXC - 1)], small_recv.at[6])
+    wait_for(dx_recv.at[pl.ds(0, NX - 1)], small_recv.at[9])
     clip_sum = dx_recv[0]
-    for j in range(1, NXC):
+    for j in range(1, NX):
         clip_sum = clip_sum + dx_recv[j]
-    for j in range(NY):
-        dy_send[j, 0:rows] = clip_sum[j * rows : (j + 1) * rows]
-        dy_send[j, rows : rows + 8] = clip_sum[group : group + 8]
-    for k in range(1, NY):
-        send(dy_send.at[lax.rem(y + k, NY)], dy_recv.at[y], 8, y_peer(k))
-    dy_recv[y] = dy_send[y]
+    for j in range(2):
+        near_send[j, 0:rows] = clip_sum[j * rows : (j + 1) * rows]
+        near_send[j, rows : 2 * rows] = clip_sum[(2 + j) * rows : (3 + j) * rows]
+    loss_y[0] = clip_sum[group : group + 8, 0:HD]
+    send(near_send.at[1 - y_lo], near_recv, 11, y_near)
+    send(loss_y.at[0], loss_y.at[1], 13, y_near)
 
     attend(1)
+
+    wait_for(near_recv, small_recv.at[11])
+    wait_for(loss_y.at[0], small_recv.at[13])
+    clip_sum = near_send[y_lo] + near_recv[...]
+    for j in range(2):
+        far_send[j] = clip_sum[j * rows : (j + 1) * rows]
+    loss_y[2] = loss_y[0] + loss_y[1]
+    send(far_send.at[1 - y_hi], far_recv, 14, y_far)
+    send(loss_y.at[2], loss_y.at[3], 15, y_far)
+
     return_head(1)
 
-    wait_for(dy_recv.at[pl.ds(0, NY - 1)], small_recv.at[8])
-    clip_sum = dy_recv[0]
-    for j in range(1, NY):
-        clip_sum = clip_sum + dy_recv[j]
-    loss_send[...] = clip_sum[rows : rows + 8, 0:HD]
+    wait_for(far_recv, small_recv.at[14])
+    wait_for(loss_y.at[0], small_recv.at[15])
+    clip_sum = far_send[y_hi] + far_recv[...]
+    loss_send[...] = loss_y[2] + loss_y[3]
     for k in range(1, NZ):
-        send(loss_send, loss_recv.at[z], 9, z_peer(k))
+        send(loss_send, loss_recv.at[z], 12, z_peer(k))
     loss_recv[z] = loss_send[...]
-    grad_clip[...] = raw_grad(clip_raw[...], clip_sum[0:rows])
-
-    wait_for(dt_recv.at[pl.ds(0, NZ - 1)], small_recv.at[7])
+    grad_clip[...] = raw_grad(clip_raw[...], clip_sum)
+
+    wait_for(dt_recv.at[pl.ds(0, NZ - 1)], small_recv.at[10])
     text_sum = dt_recv[0]
     for j in range(1, NZ):
         text_sum = text_sum + dt_recv[j]
     grad_text[...] = raw_grad(text_raw[...], text_sum)
 
-    wait_for(loss_recv.at[pl.ds(0, NZ - 1)], small_recv.at[9])
+    wait_for(loss_recv.at[pl.ds(0, NZ - 1)], small_recv.at[12])
     loss_sum = loss_recv[0]
     for j in range(1, NZ):
         loss_sum = loss_sum + loss_recv[j]
-    loss_out[0] = loss_sum[0, 0] / (rows * SEQ * BATCH)
+    loss_out[...] = loss_sum / (rows * SEQ * BATCH)
 
     for index, ref in (
         (0, clip_y.at[pl.ds(0, 3 * rows)]),
         (1, clip_y_ids.at[pl.ds(0, 3 * rows)]),
         (2, text_z.at[pl.ds(0, 3 * rows)]),
         (3, text_z_ids.at[pl.ds(0, 3 * rows)]),
-        (4, clip_x.at[pl.ds(0, 7 * group)]),
-        (5, clip_x_ids.at[pl.ds(0, 7 * group)]),
-        (6, dx_recv.at[pl.ds(0, NXC - 1)]),
-        (7, dt_recv.at[pl.ds(0, NZ - 1)]),
-        (8, dy_recv.at[pl.ds(0, NY - 1)]),
-        (9, loss_recv.at[pl.ds(0, NZ - 1)]),
+        (4, clip_x.at[pl.ds(0, 3 * group)]),
+        (5, clip_x_ids.at[pl.ds(0, 3 * group)]),
+        (6, text_c.at[pl.ds(0, group)]),
+        (7, text_c_ids.at[pl.ds(0, group)]),
+        (8, dc_recv),
+        (9, dx_recv.at[pl.ds(0, NX - 1)]),
+        (10, dt_recv.at[pl.ds(0, NZ - 1)]),
+        (11, near_recv),
+        (13, loss_y.at[0]),
+        (14, far_recv),
+        (15, loss_y.at[0]),
+        (12, loss_recv.at[pl.ds(0, NZ - 1)]),
     ):
         wait_for(ref, small_send.at[index])
     wait_sent(1)
@@ -315,6 +349,35 @@
         wait_for(ref.at[0, :, pl.ds(0, HEADS_HERE * HD)], out_local.at[a])
         wait_for(ref.at[0, :, pl.ds(0, remote)], out_send.at[a])
         wait_for(ref.at[0, :, pl.ds(0, remote)], out_recv.at[a])
+
+
+def hand_over(*refs):
+    sources, targets, (held, held_grad, held_loss, load, store) = refs[:7], refs[7:14], refs[14:]
+    size = held.shape[1] // PIECES
+    loads, stores = [], []
+
+    def through(source, middle, target):
+        index = len(loads)
+        loads.append(pltpu.make_async_copy(source, middle, load.at[index]))
+        stores.append(pltpu.make_async_copy(middle, target, store.at[index]))
+
+    for a in range(4):
+        for i in range(PIECES):
+            part = pl.ds(i * size, size)
+            through(sources[a].at[0, part], held.at[a, part], targets[a].at[0, part])
+    for a in range(2):
+        through(sources[4 + a], held_grad.at[a], targets[4 + a])
+    loss = pltpu.make_async_copy(sources[6], held_loss, load.at[len(loads)])
+    for copy in loads:
+        copy.start()
+    loss.start()
+    for arrived, copy in zip(loads, stores):
+        arrived.wait()
+        copy.start()
+    loss.wait()
+    targets[6][0] = held_loss[0, 0]
+    for copy in stores:
+        copy.wait()
 
 
 def body(queries, key_vectors, value_vectors, cotangent, clip_raw, text_raw, clip_video, text_video, logit_scale, logit_bias):
@@ -326,16 +389,16 @@
     in_smem = pl.BlockSpec(memory_space=pltpu.SMEM)
     group = NY * rows
     dma = pltpu.SemaphoreType.DMA
-    return pl.pallas_call(
+    results = pl.pallas_call(
         kernel,
         out_shape=(
             *[jax.ShapeDtypeStruct(queries.shape, BF16)] * 4,
             jax.ShapeDtypeStruct((rows, width), F32),
             jax.ShapeDtypeStruct((rows, width), F32),
-            jax.ShapeDtypeStruct((1,), F32),
+            jax.ShapeDtypeStruct((8, HD), F32),
         ),
         in_specs=[in_hbm] * 4 + [in_vmem] * 2 + [in_smem] * 4,
-        out_specs=(*[in_hbm] * 4, in_vmem, in_vmem, in_smem),
+        out_specs=(*[in_hbm] * 4, in_vmem, in_vmem, in_vmem),
         scratch_shapes=[
             pltpu.VMEM((HEADS_HERE, 4, full, HD), BF16),
             pltpu.VMEM((HEADS_HERE, 4, full, HD), BF16),
@@ -343,14 +406,21 @@
             pltpu.VMEM((full, HD), F32),
             pltpu.VMEM((group, width), BF16),
             pltpu.VMEM((group, HD), jnp.int32),
-            pltpu.VMEM((NXC * group, width), BF16),
-            pltpu.VMEM((NXC * group, HD), jnp.int32),
+            pltpu.VMEM((NX * group, width), BF16),
+            pltpu.VMEM((NX * group, HD), jnp.int32),
             pltpu.VMEM((NZ * rows, width), BF16),
             pltpu.VMEM((NZ * rows, HD), jnp.int32),
-            pltpu.VMEM((NXC, group + 8, width), F32),
-            pltpu.VMEM((NXC, group + 8, width), F32),
-            pltpu.VMEM((NY, rows + 8, width), F32),
-            pltpu.VMEM((NY, rows + 8, width), F32),
+            pltpu.VMEM((NC * NZ * rows, width), BF16),
+            pltpu.VMEM((NC * NZ * rows, HD), jnp.int32),
+            pltpu.VMEM((NC, group + 8, width), F32),
+            pltpu.VMEM((group + 8, width), F32),
+            pltpu.VMEM((NX, group + 8, width), F32),
+            pltpu.VMEM((NX, group + 8, width), F32),
+            pltpu.VMEM((2, 2 * rows, width), F32),
+            pltpu.VMEM((2 * rows, width), F32),
+            pltpu.VMEM((2, rows, width), F32),
+            pltpu.VMEM((rows, width), F32),
+            pltpu.VMEM((4, 8, HD), F32),
             pltpu.VMEM((NZ, rows, width), F32),
             pltpu.VMEM((NZ, rows, width), F32),
             pltpu.VMEM((8, HD), F32),
@@ -361,8 +431,8 @@
             dma((4,)),
             dma((4,)),
             dma((4,)),
-            dma((10,)),
-            dma((10,)),
+            dma((16,)),
+            dma((16,)),
         ],
         compiler_params=pltpu.CompilerParams(
             collective_id=0, has_side_effects=True, vmem_limit_bytes=56 * 2**20
@@ -372,6 +442,25 @@
         ),
         name="tower",
     )(queries, key_vectors, value_vectors, cotangent, clip_raw, text_raw, clip_video, text_video, logit_scale, logit_bias)
+    return pl.pallas_call(
+        hand_over,
+        out_shape=(
+            *[jax.ShapeDtypeStruct(queries.shape, BF16)] * 4,
+            jax.ShapeDtypeStruct((rows, width), F32),
+            jax.ShapeDtypeStruct((rows, width), F32),
+            jax.ShapeDtypeStruct((1,), F32),
+        ),
+        in_specs=[in_hbm] * 7,
+        out_specs=(*[in_hbm] * 6, in_smem),
+        scratch_shapes=[
+            pltpu.VMEM((4, tokens, queries.shape[2]), BF16),
+            pltpu.VMEM((2, rows, width), F32),
+            pltpu.VMEM((8, HD), F32),
+            dma((4 * PIECES + 3,)),
+            dma((4 * PIECES + 2,)),
+        ],
+        name="hand_over",
+    )(*results)
 
 
 def solution(mesh):

time: 136 us -> 91 us (0.67)
  the two profiles are of different devices: /device:TPU:17 before, /device:TPU:0 now
where the time goes in v2:
time: 91 us; the launch traced here: 90.8 us
  Pallas kernels  88.8 us (98%)
  between operations  1.94 us (2%)
    pallas_call x1, Pallas kernels, body(): pl.pallas_call(kernel, out_shape=(*[jax.ShapeDtypeStruct(queries.shape, B...  85.5 us
    pallas_call x1, Pallas kernels, body(): pl.pallas_call(hand_over, out_shape=(*[jax.ShapeDtypeStruct(queries.shape...  3.37 us

profile of v2, /device:TPU:0, one launch (start us, length us, event | category | flops | bytes accessed | tf_op | source)
XLA Modules:
  0.0 90.8 jit_solution(17223645324391824133)
XLA Ops:
  1.9 85.5 %tower.1 = (bf16[1,192,2048]{2,1,0:T(8,128)(2,1)}, bf16[1,192,2048]{2,1,0:T(8,128)(2,1)}, bf16[1,192,2048]{2,1,0:T(8,128)(2,1)}, bf16[1,192,2048]{2,1,0:T(8,128)...) custom-call(bf16[1,192,2048]{2,1,0:T(8,128)(2,1)} %q_in.1, bf16[1,192,2048]{2,1,0:T(8,128)(2,1)} %k_in.1, ...), custom_call_target="tpu_custom_call" | custom-call | flops 7247757312 | bytes 3145728 | tf_op jit(solution)/shard_map/tower/pallas_call | solution.py:392
  87.4 3.4 %hand_over.1 = (bf16[1,192,2048]{2,1,0:T(8,128)(2,1)}, bf16[1,192,2048]{2,1,0:T(8,128)(2,1)}, bf16[1,192,2048]{2,1,0:T(8,128)(2,1)}, bf16[1,192,2048]{2,1,0:T(8,...) custom-call(bf16[1,192,2048]{2,1,0:T(8,128)(2,1)} %get-tuple-element.14.refs_0_, ...), custom_call_target="tpu_custom_call" | custom-call | tf_op jit(solution)/shard_map/hand_over/pallas_call | solution.py:445

commit v3 on v2

--- a/solution.py
+++ b/solution.py
@@ -21,7 +21,6 @@
 NC = 2
 HEADS_HERE = 2
 BLOCK_Q = 512
-PIECES = 2
 
 INV_ROOT = 1.0 / math.sqrt(HD)
 EXP2_SCALE = INV_ROOT * math.log2(math.e)
@@ -67,15 +66,21 @@
 
 
 def kernel(
-    q_in, k_in, v_in, d_in, clip_raw, text_raw, clip_ids, text_ids, scale_ref, bias_ref,
+    q_in, k_in, v_in, d_in, clip_in, text_in, clip_ids_in, text_ids_in, scale_ref, bias_ref,
     o_out, dq_out, dk_out, dv_out, grad_clip, grad_text, loss_out,
-    land, res, dk_sum, dv_sum,
+    clip_ids, text_ids, load, land, res, dk_sum, dv_sum,
     clip_y, clip_y_ids, clip_x, clip_x_ids, text_z, text_z_ids, text_c, text_c_ids,
-    dc_send, dc_recv, dx_send, dx_recv, near_send, near_recv, far_send, far_recv, loss_y, dt_send, dt_recv, loss_send, loss_recv,
+    dc_send, dc_recv, dx_send, dx_recv, near_send, near_recv, far_send, far_recv, loss_y, dt_send, dt_recv, loss_recv,
     in_send, in_recv, in_local, out_send, out_recv, out_local, small_send, small_recv,
 ):
     tokens = q_in.shape[1]
-    rows = clip_raw.shape[0]
+    rows = clip_in.shape[0]
+    scalars = [
+        pltpu.make_async_copy(clip_ids_in, clip_ids, load.at[2]),
+        pltpu.make_async_copy(text_ids_in, text_ids, load.at[3]),
+    ]
+    for copy in scalars:
+        copy.start()
     full = tokens * SEQ
     s = lax.axis_index("seq")
     b = lax.axis_index("batch")
@@ -113,10 +118,16 @@
     greet(y_peer(1))
     greet(y_peer(3))
 
-    clip_y[aligned(y, rows), :] = unit_rows(clip_raw[...])[0].astype(BF16)
-    text_z[aligned(z, rows), :] = unit_rows(text_raw[...])[0].astype(BF16)
+    for copy in scalars:
+        copy.wait()
     clip_y_ids[aligned(y, rows), :] = column_of_ids(clip_ids, rows)
     text_z_ids[aligned(z, rows), :] = column_of_ids(text_ids, rows)
+    clip_own = aligned(y, rows)
+    text_own = aligned(z, rows)
+    clip_load = pltpu.make_async_copy(clip_in, clip_y.at[clip_own], load.at[0])
+    text_load = pltpu.make_async_copy(text_in, text_z.at[text_own], load.at[1])
+    clip_load.start()
+    text_load.start()
 
     pl.semaphore_wait(barrier, SEQ - 1 + NX - 1 + 3)
 
@@ -127,13 +138,11 @@
         ).start()
 
     for k in range(1, NY):
-        mine = aligned(y, rows)
-        send(clip_y.at[mine], clip_y.at[mine], 0, y_peer(k))
-        send(clip_y_ids.at[mine], clip_y_ids.at[mine], 1, y_peer(k))
+        send(clip_in, clip_y.at[clip_own], 0, y_peer(k))
+        send(clip_y_ids.at[clip_own], clip_y_ids.at[clip_own], 1, y_peer(k))
     for k in range(1, NZ):
-        mine = aligned(z, rows)
-        send(text_z.at[mine], text_z.at[mine], 2, z_peer(k))
-        send(text_z_ids.at[mine], text_z_ids.at[mine], 3, z_peer(k))
+        send(text_in, text_z.at[text_own], 2, z_peer(k))
+        send(text_z_ids.at[text_own], text_z_ids.at[text_own], 3, z_peer(k))
 
     ins = (k_in, q_in, v_in, d_in)
 
@@ -174,6 +183,8 @@
     send_head(0)
 
     group = NY * rows
+    clip_load.wait()
+    text_load.wait()
     for k in range(1, NX):
         send(clip_y, clip_x.at[aligned(x, group)], 4, x_peer(k))
         send(clip_y_ids, clip_x_ids.at[aligned(x, group)], 5, x_peer(k))
@@ -190,8 +201,8 @@
     wait_for(clip_x_ids.at[pl.ds(0, 3 * group)], small_recv.at[5])
     scale = scale_ref[0]
     offset = bias_ref[0]
-    clip_all = clip_x[...]
-    text_all = text_c[...]
+    clip_all = unit_rows(clip_x[...])[0].astype(BF16)
+    text_all = unit_rows(text_c[...])[0].astype(BF16)
     logits = scale * nt(clip_all, text_all) + offset
     text_row = jnp.transpose(text_c_ids[...].astype(F32))[0:1, :]
     sign = jnp.where(clip_x_ids[...].astype(F32) == text_row, F32(1.0), F32(-1.0))
@@ -297,30 +308,26 @@
     clip_sum = near_send[y_lo] + near_recv[...]
     for j in range(2):
         far_send[j] = clip_sum[j * rows : (j + 1) * rows]
-    loss_y[2] = loss_y[0] + loss_y[1]
+    loss_recv[s] = loss_y[0] + loss_y[1]
     send(far_send.at[1 - y_hi], far_recv, 14, y_far)
-    send(loss_y.at[2], loss_y.at[3], 15, y_far)
+    for k in range(1, SEQ):
+        send(loss_recv.at[s], loss_recv.at[s], 12, seq_peer(k))
 
     return_head(1)
 
     wait_for(far_recv, small_recv.at[14])
-    wait_for(loss_y.at[0], small_recv.at[15])
     clip_sum = far_send[y_hi] + far_recv[...]
-    loss_send[...] = loss_y[2] + loss_y[3]
-    for k in range(1, NZ):
-        send(loss_send, loss_recv.at[z], 12, z_peer(k))
-    loss_recv[z] = loss_send[...]
-    grad_clip[...] = raw_grad(clip_raw[...], clip_sum)
+    grad_clip[...] = raw_grad(clip_y[clip_own, :], clip_sum)
 
     wait_for(dt_recv.at[pl.ds(0, NZ - 1)], small_recv.at[10])
     text_sum = dt_recv[0]
     for j in range(1, NZ):
         text_sum = text_sum + dt_recv[j]
-    grad_text[...] = raw_grad(text_raw[...], text_sum)
-
-    wait_for(loss_recv.at[pl.ds(0, NZ - 1)], small_recv.at[12])
+    grad_text[...] = raw_grad(text_z[text_own, :], text_sum)
+
+    wait_for(loss_recv.at[pl.ds(0, SEQ - 1)], small_recv.at[12])
     loss_sum = loss_recv[0]
-    for j in range(1, NZ):
+    for j in range(1, SEQ):
         loss_sum = loss_sum + loss_recv[j]
     loss_out[...] = loss_sum / (rows * SEQ * BATCH)
 
@@ -339,8 +346,7 @@
         (11, near_recv),
         (13, loss_y.at[0]),
         (14, far_recv),
-        (15, loss_y.at[0]),
-        (12, loss_recv.at[pl.ds(0, NZ - 1)]),
+        (12, loss_recv.at[pl.ds(0, SEQ - 1)]),
     ):
         wait_for(ref, small_send.at[index])
     wait_sent(1)
@@ -352,31 +358,12 @@
 
 
 def hand_over(*refs):
-    sources, targets, (held, held_grad, held_loss, load, store) = refs[:7], refs[7:14], refs[14:]
-    size = held.shape[1] // PIECES
-    loads, stores = [], []
-
-    def through(source, middle, target):
-        index = len(loads)
-        loads.append(pltpu.make_async_copy(source, middle, load.at[index]))
-        stores.append(pltpu.make_async_copy(middle, target, store.at[index]))
-
-    for a in range(4):
-        for i in range(PIECES):
-            part = pl.ds(i * size, size)
-            through(sources[a].at[0, part], held.at[a, part], targets[a].at[0, part])
-    for a in range(2):
-        through(sources[4 + a], held_grad.at[a], targets[4 + a])
-    loss = pltpu.make_async_copy(sources[6], held_loss, load.at[len(loads)])
-    for copy in loads:
+    sources, targets, sems = refs[:7], refs[7:14], refs[14]
+    copies = [pltpu.make_async_copy(sources[a], targets[a], sems.at[a]) for a in range(6)]
+    for copy in copies:
         copy.start()
-    loss.start()
-    for arrived, copy in zip(loads, stores):
-        arrived.wait()
-        copy.start()
-    loss.wait()
-    targets[6][0] = held_loss[0, 0]
-    for copy in stores:
+    targets[6][0] = sources[6][0, 0]
+    for copy in copies:
         copy.wait()
 
 
@@ -389,17 +376,21 @@
     in_smem = pl.BlockSpec(memory_space=pltpu.SMEM)
     group = NY * rows
     dma = pltpu.SemaphoreType.DMA
+    in_place = (queries, key_vectors, value_vectors, cotangent, clip_raw, text_raw, clip_video, text_video)
     results = pl.pallas_call(
         kernel,
         out_shape=(
-            *[jax.ShapeDtypeStruct(queries.shape, BF16)] * 4,
-            jax.ShapeDtypeStruct((rows, width), F32),
-            jax.ShapeDtypeStruct((rows, width), F32),
-            jax.ShapeDtypeStruct((8, HD), F32),
+            *[pltpu.VMEM(queries.shape, BF16)] * 4,
+            pltpu.VMEM((rows, width), F32),
+            pltpu.VMEM((rows, width), F32),
+            pltpu.VMEM((8, HD), F32),
         ),
-        in_specs=[in_hbm] * 4 + [in_vmem] * 2 + [in_smem] * 4,
-        out_specs=(*[in_hbm] * 4, in_vmem, in_vmem, in_vmem),
+        in_specs=[in_hbm] * 8 + [in_smem] * 2,
+        out_specs=[in_vmem] * 7,
         scratch_shapes=[
+            pltpu.SMEM((rows,), jnp.int32),
+            pltpu.SMEM((rows,), jnp.int32),
+            dma((4,)),
             pltpu.VMEM((HEADS_HERE, 4, full, HD), BF16),
             pltpu.VMEM((HEADS_HERE, 4, full, HD), BF16),
             pltpu.VMEM((full, HD), F32),
@@ -420,28 +411,27 @@
             pltpu.VMEM((2 * rows, width), F32),
             pltpu.VMEM((2, rows, width), F32),
             pltpu.VMEM((rows, width), F32),
-            pltpu.VMEM((4, 8, HD), F32),
+            pltpu.VMEM((2, 8, HD), F32),
             pltpu.VMEM((NZ, rows, width), F32),
             pltpu.VMEM((NZ, rows, width), F32),
-            pltpu.VMEM((8, HD), F32),
-            pltpu.VMEM((NZ, 8, HD), F32),
+            pltpu.VMEM((SEQ, 8, HD), F32),
             dma((HEADS_HERE, 4)),
             dma((HEADS_HERE, 4)),
             dma((HEADS_HERE, 4)),
             dma((4,)),
             dma((4,)),
             dma((4,)),
-            dma((16,)),
-            dma((16,)),
+            dma((15,)),
+            dma((15,)),
         ],
         compiler_params=pltpu.CompilerParams(
-            collective_id=0, has_side_effects=True, vmem_limit_bytes=56 * 2**20
+            collective_id=0, has_side_effects=True, vmem_limit_bytes=48 * 2**20
         ),
         cost_estimate=pl.CostEstimate(
             flops=HEADS_HERE * 12 * full * full * HD, bytes_accessed=8 * full * HD * 2, transcendentals=HEADS_HERE * full * full
         ),
         name="tower",
-    )(queries, key_vectors, value_vectors, cotangent, clip_raw, text_raw, clip_video, text_video, logit_scale, logit_bias)
+    )(*[pltpu.with_memory_space_constraint(array, pltpu.HBM) for array in in_place], logit_scale, logit_bias)
     return pl.pallas_call(
         hand_over,
         out_shape=(
@@ -450,17 +440,11 @@
             jax.ShapeDtypeStruct((rows, width), F32),
             jax.ShapeDtypeStruct((1,), F32),
         ),
-        in_specs=[in_hbm] * 7,
+        in_specs=[in_vmem] * 7,
         out_specs=(*[in_hbm] * 6, in_smem),
-        scratch_shapes=[
-            pltpu.VMEM((4, tokens, queries.shape[2]), BF16),
-            pltpu.VMEM((2, rows, width), F32),
-            pltpu.VMEM((8, HD), F32),
-            dma((4 * PIECES + 3,)),
-            dma((4 * PIECES + 2,)),
-        ],
+        scratch_shapes=[dma((6,))],
         name="hand_over",
-    )(*results)
+    )(*[pltpu.with_memory_space_constraint(array, pltpu.VMEM) for array in results])
 
 
 def solution(mesh):

time: 91 us -> 88.8 us (0.976)
  Pallas kernels: 88.8 us -> 86.7 us
    pallas_call x1, Pallas kernels: 3.37 us -> 2.24 us  [body(): pl.pallas_call(hand_over, out_shape=(*[jax.ShapeDtypeStruct(queries.shape...]
    pallas_call x1, Pallas kernels: 85.5 us -> 84.5 us  [body(): pl.pallas_call(kernel, out_shape=(*[pltpu.VMEM(queries.shape, BF16)] * 4,...]
where the time goes in v3:
time: 88.8 us; the launch traced here: 88.6 us
  Pallas kernels  86.7 us (98%)
  between operations  1.94 us (2%)
    pallas_call x1, Pallas kernels, body(): pl.pallas_call(kernel, out_shape=(*[pltpu.VMEM(queries.shape, BF16)] * 4,...  84.5 us
    pallas_call x1, Pallas kernels, body(): pl.pallas_call(hand_over, out_shape=(*[jax.ShapeDtypeStruct(queries.shape...  2.24 us

profile of v3, /device:TPU:0, one launch (start us, length us, event | category | flops | bytes accessed | tf_op | source)
XLA Modules:
  0.0 88.6 jit_solution(10997820499826111722)
XLA Ops:
  1.9 84.5 %tower.1 = (bf16[1,192,2048]{2,1,0:T(8,128)(2,1)S(1)}, bf16[1,192,2048]{2,1,0:T(8,128)(2,1)S(1)}, bf16[1,192,2048]{2,1,0:T(8,128)(2,1)S(1)}, bf16[1,192,2048]{2,...) custom-call(bf16[1,192,2048]{2,1,0:T(8,128)(2,1)} %q_in.1, ...), custom_call_target="tpu_custom_call" | custom-call | flops 7247757312 | bytes 3145728 | tf_op jit(solution)/shard_map/tower/pallas_call | solution.py:380
  86.4 2.2 %hand_over.1 = (bf16[1,192,2048]{2,1,0:T(8,128)(2,1)}, bf16[1,192,2048]{2,1,0:T(8,128)(2,1)}, bf16[1,192,2048]{2,1,0:T(8,128)(2,1)}, bf16[1,192,2048]{2,1,0:T(8,...) custom-call(bf16[1,192,2048]{2,1,0:T(8,128)(2,1)S(1)} %get-tuple-element.14.refs_0_, ...), custom_call_target="tpu_custom_call" | custom-call | tf_op jit(solution)/shard_map/hand_over/pallas_call | solution.py:435

commit v4 on v3

--- a/solution.py
+++ b/solution.py
@@ -48,9 +48,13 @@
     return (rawf / norm, norm)
 
 
+def across(unit, direction):
+    return direction - unit * jnp.sum(unit * direction, axis=1, keepdims=True)
+
+
 def raw_grad(raw, direction):
     unit, norm = unit_rows(raw)
-    return (direction - unit * jnp.sum(unit * direction, axis=1, keepdims=True)) / norm
+    return across(unit, direction) / norm
 
 
 def wait_for(ref, sem):
@@ -70,7 +74,7 @@
     o_out, dq_out, dk_out, dv_out, grad_clip, grad_text, loss_out,
     clip_ids, text_ids, load, land, res, dk_sum, dv_sum,
     clip_y, clip_y_ids, clip_x, clip_x_ids, text_z, text_z_ids, text_c, text_c_ids,
-    dc_send, dc_recv, dx_send, dx_recv, near_send, near_recv, far_send, far_recv, loss_y, dt_send, dt_recv, loss_recv,
+    dc_send, dc_recv, dx_send, dx_recv, near_own, near_send, near_recv, far_own, far_send, far_recv, loss_y, dt_own, dt_send, dt_recv, loss_recv,
     in_send, in_recv, in_local, out_send, out_recv, out_local, small_send, small_recv,
 ):
     tokens = q_in.shape[1]
@@ -221,8 +225,10 @@
         dx_send[j, 0:group] = clip_part[j * group : (j + 1) * group]
     wait_for(dc_recv, small_recv.at[8])
     text_sum = dc_send[c] + dc_recv[...]
+    text_across = across(unit_rows(text_z[...])[0], text_sum[0:group])
     for j in range(NZ):
-        dt_send[j] = text_sum[j * rows : (j + 1) * rows]
+        dt_own[j] = text_across[j * rows : (j + 1) * rows]
+        dt_send[j] = dt_own[j].astype(BF16)
     for j in range(NX):
         dx_send[j, group : group + 8] = text_sum[group : group + 8]
     for k in range(1, NX):
@@ -230,7 +236,7 @@
     for k in range(1, NZ):
         send(dt_send.at[lax.rem(z + k, NZ)], dt_recv.at[z], 10, z_peer(k))
     dx_recv[x] = dx_send[x]
-    dt_recv[z] = dt_send[z]
+    dt_recv[z] = jnp.zeros(dt_recv.shape[1:], BF16)
 
     wait_sent(0)
     send_head(1)
@@ -294,9 +300,11 @@
     clip_sum = dx_recv[0]
     for j in range(1, NX):
         clip_sum = clip_sum + dx_recv[j]
+    clip_across = across(unit_rows(clip_y[...])[0], clip_sum[0:group])
     for j in range(2):
-        near_send[j, 0:rows] = clip_sum[j * rows : (j + 1) * rows]
-        near_send[j, rows : 2 * rows] = clip_sum[(2 + j) * rows : (3 + j) * rows]
+        near_own[j, 0:rows] = clip_across[j * rows : (j + 1) * rows]
+        near_own[j, rows : 2 * rows] = clip_across[(2 + j) * rows : (3 + j) * rows]
+        near_send[j] = near_own[j].astype(BF16)
     loss_y[0] = clip_sum[group : group + 8, 0:HD]
     send(near_send.at[1 - y_lo], near_recv, 11, y_near)
     send(loss_y.at[0], loss_y.at[1], 13, y_near)
@@ -305,9 +313,10 @@
 
     wait_for(near_recv, small_recv.at[11])
     wait_for(loss_y.at[0], small_recv.at[13])
-    clip_sum = near_send[y_lo] + near_recv[...]
+    clip_sum = near_own[y_lo] + near_recv[...].astype(F32)
     for j in range(2):
-        far_send[j] = clip_sum[j * rows : (j + 1) * rows]
+        far_own[j] = clip_sum[j * rows : (j + 1) * rows]
+        far_send[j] = far_own[j].astype(BF16)
     loss_recv[s] = loss_y[0] + loss_y[1]
     send(far_send.at[1 - y_hi], far_recv, 14, y_far)
     for k in range(1, SEQ):
@@ -316,13 +325,13 @@
     return_head(1)
 
     wait_for(far_recv, small_recv.at[14])
-    clip_sum = far_send[y_hi] + far_recv[...]
+    clip_sum = far_own[y_hi] + far_recv[...].astype(F32)
     grad_clip[...] = raw_grad(clip_y[clip_own, :], clip_sum)
 
     wait_for(dt_recv.at[pl.ds(0, NZ - 1)], small_recv.at[10])
-    text_sum = dt_recv[0]
-    for j in range(1, NZ):
-        text_sum = text_sum + dt_recv[j]
+    text_sum = dt_own[z]
+    for j in range(NZ):
+        text_sum = text_sum + dt_recv[j].astype(F32)
     grad_text[...] = raw_grad(text_z[text_own, :], text_sum)
 
     wait_for(loss_recv.at[pl.ds(0, SEQ - 1)], small_recv.at[12])
@@ -408,12 +417,15 @@
             pltpu.VMEM((NX, group + 8, width), F32),
             pltpu.VMEM((NX, group + 8, width), F32),
             pltpu.VMEM((2, 2 * rows, width), F32),
-            pltpu.VMEM((2 * rows, width), F32),
+            pltpu.VMEM((2, 2 * rows, width), BF16),
+            pltpu.VMEM((2 * rows, width), BF16),
             pltpu.VMEM((2, rows, width), F32),
-            pltpu.VMEM((rows, width), F32),
+            pltpu.VMEM((2, rows, width), BF16),
+            pltpu.VMEM((rows, width), BF16),
             pltpu.VMEM((2, 8, HD), F32),
             pltpu.VMEM((NZ, rows, width), F32),
-            pltpu.VMEM((NZ, rows, width), F32),
+            pltpu.VMEM((NZ, rows, width), BF16),
+            pltpu.VMEM((NZ, rows, width), BF16),
             pltpu.VMEM((SEQ, 8, HD), F32),
             dma((HEADS_HERE, 4)),
             dma((HEADS_HERE, 4)),

time: 88.8 us -> 87.5 us (0.985)
  Pallas kernels: 86.7 us -> 85.5 us
    pallas_call x1, Pallas kernels: 84.5 us -> 83.2 us  [body(): pl.pallas_call(kernel, out_shape=(*[pltpu.VMEM(queries.shape, BF16)] * 4,...]
where the time goes in v4:
time: 87.5 us; the launch traced here: 87.4 us
  Pallas kernels  85.5 us (98%)
  between operations  1.94 us (2%)
    pallas_call x1, Pallas kernels, body(): pl.pallas_call(kernel, out_shape=(*[pltpu.VMEM(queries.shape, BF16)] * 4,...  83.2 us
    pallas_call x1, Pallas kernels, body(): pl.pallas_call(hand_over, out_shape=(*[jax.ShapeDtypeStruct(queries.shape...  2.24 us

profile of v4, /device:TPU:0, one launch (start us, length us, event | category | flops | bytes accessed | tf_op | source)
XLA Modules:
  0.0 87.4 jit_solution(3997383749771179490)
XLA Ops:
  1.9 83.2 %tower.1 = (bf16[1,192,2048]{2,1,0:T(8,128)(2,1)S(1)}, bf16[1,192,2048]{2,1,0:T(8,128)(2,1)S(1)}, bf16[1,192,2048]{2,1,0:T(8,128)(2,1)S(1)}, bf16[1,192,2048]{2,...) custom-call(bf16[1,192,2048]{2,1,0:T(8,128)(2,1)} %q_in.1, ...), custom_call_target="tpu_custom_call" | custom-call | flops 7247757312 | bytes 3145728 | tf_op jit(solution)/shard_map/tower/pallas_call | solution.py:389
  85.1 2.2 %hand_over.1 = (bf16[1,192,2048]{2,1,0:T(8,128)(2,1)}, bf16[1,192,2048]{2,1,0:T(8,128)(2,1)}, bf16[1,192,2048]{2,1,0:T(8,128)(2,1)}, bf16[1,192,2048]{2,1,0:T(8,...) custom-call(bf16[1,192,2048]{2,1,0:T(8,128)(2,1)S(1)} %get-tuple-element.14.refs_0_, ...), custom_call_target="tpu_custom_call" | custom-call | tf_op jit(solution)/shard_map/hand_over/pallas_call | solution.py:447

commit v5 on v4

--- a/solution.py
+++ b/solution.py
@@ -367,11 +367,13 @@
 
 
 def hand_over(*refs):
-    sources, targets, sems = refs[:7], refs[7:14], refs[14]
+    sources, targets, loss, sems = refs[:7], refs[7:14], refs[14], refs[15]
     copies = [pltpu.make_async_copy(sources[a], targets[a], sems.at[a]) for a in range(6)]
     for copy in copies:
         copy.start()
-    targets[6][0] = sources[6][0, 0]
+    loss[0] = sources[6][0, 0]
+    copies.append(pltpu.make_async_copy(loss, targets[6], sems.at[6]))
+    copies[-1].start()
     for copy in copies:
         copy.wait()
 
@@ -453,8 +455,8 @@
             jax.ShapeDtypeStruct((1,), F32),
         ),
         in_specs=[in_vmem] * 7,
-        out_specs=(*[in_hbm] * 6, in_smem),
-        scratch_shapes=[dma((6,))],
+        out_specs=[in_hbm] * 7,
+        scratch_shapes=[pltpu.SMEM((1,), F32), dma((7,))],
         name="hand_over",
     )(*[pltpu.with_memory_space_constraint(array, pltpu.VMEM) for array in results])
 

time: 87.5 us -> 87 us (level)
  no operation moved by 1% of the time
where the time goes in v5:
time: 87 us; the launch traced here: 86.9 us
  Pallas kernels  85 us (98%)
  between operations  1.94 us (2%)
    pallas_call x1, Pallas kernels, body(): pl.pallas_call(kernel, out_shape=(*[pltpu.VMEM(queries.shape, BF16)] * 4,...  83.2 us
    pallas_call x1, Pallas kernels, body(): pl.pallas_call(hand_over, out_shape=(*[jax.ShapeDtypeStruct(queries.shape...  1.75 us

profile of v5, /device:TPU:0, one launch (start us, length us, event | category | flops | bytes accessed | tf_op | source)
XLA Modules:
  0.0 86.9 jit_solution(4239678322936229946)
XLA Ops:
  1.9 83.2 %tower.1 = (bf16[1,192,2048]{2,1,0:T(8,128)(2,1)S(1)}, bf16[1,192,2048]{2,1,0:T(8,128)(2,1)S(1)}, bf16[1,192,2048]{2,1,0:T(8,128)(2,1)S(1)}, bf16[1,192,2048]{2,...) custom-call(bf16[1,192,2048]{2,1,0:T(8,128)(2,1)} %q_in.1, ...), custom_call_target="tpu_custom_call" | custom-call | flops 7247757312 | bytes 3145728 | tf_op jit(solution)/shard_map/tower/pallas_call | solution.py:391
  85.1 1.7 %hand_over.1 = (bf16[1,192,2048]{2,1,0:T(8,128)(2,1)}, bf16[1,192,2048]{2,1,0:T(8,128)(2,1)}, bf16[1,192,2048]{2,1,0:T(8,128)(2,1)}, bf16[1,192,2048]{2,1,0:T(8,...) custom-call(bf16[1,192,2048]{2,1,0:T(8,128)(2,1)S(1)} %get-tuple-element.14.refs_0_, ...), custom_call_target="tpu_custom_call" | custom-call | tf_op jit(solution)/shard_map/hand_over/pallas_call | solution.py:449

commit v6 on v5

--- a/solution.py
+++ b/solution.py
@@ -181,8 +181,6 @@
 
     wait_for(clip_y.at[pl.ds(0, 3 * rows)], small_recv.at[0])
     wait_for(clip_y_ids.at[pl.ds(0, 3 * rows)], small_recv.at[1])
-    wait_for(text_z.at[pl.ds(0, 3 * rows)], small_recv.at[2])
-    wait_for(text_z_ids.at[pl.ds(0, 3 * rows)], small_recv.at[3])
 
     send_head(0)
 
@@ -194,6 +192,8 @@
         send(clip_y_ids, clip_x_ids.at[aligned(x, group)], 5, x_peer(k))
     clip_x[aligned(x, group), :] = clip_y[...]
     clip_x_ids[aligned(x, group), :] = clip_y_ids[...]
+    wait_for(text_z.at[pl.ds(0, 3 * rows)], small_recv.at[2])
+    wait_for(text_z_ids.at[pl.ds(0, 3 * rows)], small_recv.at[3])
     send(text_z, text_c.at[aligned(c, group)], 6, c_peer)
     send(text_z_ids, text_c_ids.at[aligned(c, group)], 7, c_peer)
     text_c[aligned(c, group), :] = text_z[...]

time: 87 us -> 86.9 us (level)
  no operation moved by 1% of the time
where the time goes in v6:
time: 86.9 us; the launch traced here: 86.6 us
  Pallas kernels  84.7 us (97%)
  between operations  1.94 us (2%)
    pallas_call x1, Pallas kernels, body(): pl.pallas_call(kernel, out_shape=(*[pltpu.VMEM(queries.shape, BF16)] * 4,...  82.9 us
    pallas_call x1, Pallas kernels, body(): pl.pallas_call(hand_over, out_shape=(*[jax.ShapeDtypeStruct(queries.shape...  1.75 us

profile of v6, /device:TPU:0, one launch (start us, length us, event | category | flops | bytes accessed | tf_op | source)
XLA Modules:
  0.0 86.6 jit_solution(4261629668975412785)
XLA Ops:
  1.9 82.9 %tower.1 = (bf16[1,192,2048]{2,1,0:T(8,128)(2,1)S(1)}, bf16[1,192,2048]{2,1,0:T(8,128)(2,1)S(1)}, bf16[1,192,2048]{2,1,0:T(8,128)(2,1)S(1)}, bf16[1,192,2048]{2,...) custom-call(bf16[1,192,2048]{2,1,0:T(8,128)(2,1)} %q_in.1, ...), custom_call_target="tpu_custom_call" | custom-call | flops 7247757312 | bytes 3145728 | tf_op jit(solution)/shard_map/tower/pallas_call | solution.py:391
  84.9 1.7 %hand_over.1 = (bf16[1,192,2048]{2,1,0:T(8,128)(2,1)}, bf16[1,192,2048]{2,1,0:T(8,128)(2,1)}, bf16[1,192,2048]{2,1,0:T(8,128)(2,1)}, bf16[1,192,2048]{2,1,0:T(8,...) custom-call(bf16[1,192,2048]{2,1,0:T(8,128)(2,1)S(1)} %get-tuple-element.14.refs_0_, ...), custom_call_target="tpu_custom_call" | custom-call | tf_op jit(solution)/shard_map/hand_over/pallas_call | solution.py:449

commit v7 on v6

--- a/solution.py
+++ b/solution.py
@@ -158,7 +158,7 @@
             ).start()
 
             def to_peer(k, carry):
-                peer = seq_peer(k)
+                peer = (k + jnp.where(k >= s, 1, 0), b)
                 pltpu.make_async_remote_copy(
                     src_ref=ref.at[0, :, aligned(peer[0] * HEADS_HERE + h, HD)],
                     dst_ref=land.at[h, a, mine],
@@ -167,7 +167,7 @@
                 ).start()
                 return carry
 
-            lax.fori_loop(1, SEQ, to_peer, 0)
+            lax.fori_loop(0, SEQ - 1, to_peer, 0)
 
     others = full - tokens
 
@@ -282,7 +282,7 @@
             ).start()
 
             def to_peer(k, carry):
-                peer = seq_peer(k)
+                peer = (k + jnp.where(k >= s, 1, 0), b)
                 pltpu.make_async_remote_copy(
                     src_ref=res.at[h, a, aligned(peer[0], tokens)],
                     dst_ref=ref.at[0, :, columns],
@@ -291,7 +291,7 @@
                 ).start()
                 return carry
 
-            lax.fori_loop(1, SEQ, to_peer, 0)
+            lax.fori_loop(0, SEQ - 1, to_peer, 0)
 
     attend(0)
     return_head(0)

time: 86.9 us -> 86.8 us (level)
  no operation moved by 1% of the time
where the time goes in v7:
time: 86.8 us; the launch traced here: 86.4 us
  Pallas kernels  84.4 us (97%)
  between operations  1.94 us (2%)
    pallas_call x1, Pallas kernels, body(): pl.pallas_call(kernel, out_shape=(*[pltpu.VMEM(queries.shape, BF16)] * 4,...  82.7 us
    pallas_call x1, Pallas kernels, body(): pl.pallas_call(hand_over, out_shape=(*[jax.ShapeDtypeStruct(queries.shape...  1.75 us

profile of v7, /device:TPU:0, one launch (start us, length us, event | category | flops | bytes accessed | tf_op | source)
XLA Modules:
  0.0 86.4 jit_solution(4431627030598747751)
XLA Ops:
  1.9 82.7 %tower.1 = (bf16[1,192,2048]{2,1,0:T(8,128)(2,1)S(1)}, bf16[1,192,2048]{2,1,0:T(8,128)(2,1)S(1)}, bf16[1,192,2048]{2,1,0:T(8,128)(2,1)S(1)}, bf16[1,192,2048]{2,...) custom-call(bf16[1,192,2048]{2,1,0:T(8,128)(2,1)} %q_in.1, ...), custom_call_target="tpu_custom_call" | custom-call | flops 7247757312 | bytes 3145728 | tf_op jit(solution)/shard_map/tower/pallas_call | solution.py:391
  84.6 1.7 %hand_over.1 = (bf16[1,192,2048]{2,1,0:T(8,128)(2,1)}, bf16[1,192,2048]{2,1,0:T(8,128)(2,1)}, bf16[1,192,2048]{2,1,0:T(8,128)(2,1)}, bf16[1,192,2048]{2,1,0:T(8,...) custom-call(bf16[1,192,2048]{2,1,0:T(8,128)(2,1)S(1)} %get-tuple-element.14.refs_0_, ...), custom_call_target="tpu_custom_call" | custom-call | tf_op jit(solution)/shard_map/hand_over/pallas_call | solution.py:449
